TPU v7x, 512 devices: a whole 4x8x8 slice. The times are simulated.
512 devices in a mesh: frame: 16 (over y, x_lo), row: 32 (over x_hi, z, core).
Axes of the slice: x: 4 (x_hi: 2, x_lo: 2; x = x_hi * 2 + x_lo), y: 8, z: 8, core: 2. Of those that a mesh axis runs over, the one named last changes fastest.
Arguments:
- queries: bfloat16 [16, 32, 128, 1536], P('frame', 'row'), may hold values from -100 to 100
- keys: bfloat16 [16, 32, 256, 1536], P('frame', 'row'), may hold values from -5 to 5
- values: bfloat16 [16, 32, 256, 1536], P('frame', 'row'), may hold values from -24 to 24
- pad_counts: int32 [16, 32], replicated, may hold values from 0 to 192, as said below
Outputs:
- attended: bfloat16 [16, 32, 128, 1536], P('frame', 'row')
Inputs may be any that keep to these rules, and one draw needn't show every extreme that they name: `pad_counts`: each entry counts padded tokens of one tile; the value 3 * 64 and the value 0 each occur in every draw.
All inputs are finite; a program needn't handle non-finite values.
Results may differ from a plain program's by a relative error of at most 0.0049.
Values may be sent and summed in bfloat16 or wider, within the bound.
A program may use at most 64 MiB of HBM per device.

v0:
```python
import jax
import jax.numpy as jnp
from jax import lax
from jax.sharding import PartitionSpec as P

H = 12
HDIM = 128
TILE = 256
QROWS = 128
RT = 4


def passed_along(shard, axis, by):
    peers = lax.axis_size(axis)
    pairs = [(i, i + by) for i in range(peers) if 0 <= i + by < peers]
    return lax.ppermute(shard, axis, pairs)


def attend_stack(local_queries, near_pairs, near_pads):
    width = H * HDIM
    position = jnp.arange(TILE, dtype=jnp.int32)
    live = (position[None, None, :] < TILE - near_pads[..., None]).reshape(-1)
    flat_pairs = near_pairs.reshape(-1, 2 * width)
    scale = HDIM ** (-0.5)

    def one_head(head):
        query_head = lax.dynamic_slice_in_dim(local_queries, head * HDIM, HDIM, 1)
        key_head = lax.dynamic_slice_in_dim(flat_pairs, head * HDIM, HDIM, 1)
        value_head = lax.dynamic_slice_in_dim(flat_pairs, width + head * HDIM, HDIM, 1)
        scores = (
            lax.dot_general(
                query_head, key_head, (((1,), (1,)), ((), ())), preferred_element_type=jnp.float32
            )
            * scale
        )
        scores = jnp.where(live[None, :], scores, jnp.float32(-1e30))
        top_score = jnp.max(scores, axis=1, keepdims=True)
        expo = jnp.exp(scores - top_score)
        total = jnp.sum(expo, axis=1, keepdims=True)
        weights = (expo / total).astype(jnp.bfloat16)
        return jnp.dot(weights, value_head, preferred_element_type=jnp.float32)

    heads_out = lax.map(one_head, jnp.arange(H, dtype=jnp.int32))
    rows = local_queries.shape[0]
    return jnp.transpose(heads_out, (1, 0, 2)).reshape(rows, width).astype(jnp.bfloat16)


def shards(queries, keys, values, pad_counts):
    width = H * HDIM
    frame_count = lax.axis_size("frame")
    row_count = lax.axis_size("row")
    column_tiles = row_count // RT
    pairs = jnp.concatenate((keys, values), axis=-1)
    layers = []
    for step_frame in (-1, 0, 1):
        across = []
        for step_row in (-1, 0, 1):
            if step_frame == 0 and step_row == 0:
                across.append(pairs)
            else:
                offset = -(step_frame * row_count + step_row * column_tiles)
                across.append(passed_along(pairs, ("frame", "row"), offset))
        layers.append(jnp.concatenate(across, axis=1))
    near_pairs = jnp.concatenate(layers, axis=0)
    padded_pads = jnp.pad(
        pad_counts.reshape(frame_count, RT, column_tiles),
        ((1, 1), (1, 1), (0, 0)),
        constant_values=TILE,
    )
    frame_index = lax.axis_index("frame")
    row_index = lax.axis_index("row")
    row_tile = row_index // column_tiles
    column_tile = row_index % column_tiles
    near_pads = lax.dynamic_slice(
        padded_pads, (frame_index, row_tile, column_tile), (3, 3, 1)
    ).reshape(3, 3)
    result = attend_stack(queries[0, 0], near_pairs, near_pads)
    return result.reshape(1, 1, QROWS, width)


def solution(mesh):
    in_specs = (
        P("frame", "row", None, None),
        P("frame", "row", None, None),
        P("frame", "row", None, None),
        P(),
    )
    out_specs = P("frame", "row", None, None)
    return jax.shard_map(shards, mesh=mesh, in_specs=in_specs, out_specs=out_specs, check_vma=False)
```

profile of v0, /device:TPU:392, one launch (start us, length us, event | category | flops | bytes accessed | tf_op | source)
XLA Modules:
  0.0 588.8 jit_solution(11436646679339496735)
XLA Ops:
  0.0 1.3 constant_dynamic-update-slice_fusion.1
  1.5 2.8 collective-permute-start
  4.3 3.1 collective-permute-start.1
  7.5 9.1 %collective-permute-start.2 = (bf16[1,1,256,3072]{3,2,1,0:T(8,128)(2,1)S(1)}, bf16[1,1,256,3072]{3,2,1,0:T(8,128)(2,1)S(1)}, u32[]{:S(2)}, u32[]{:S(2)}) collective-permute-start(bf16[1,1,256,3072]{3,2,1,0:T(8,128)(2,1)S(1)} %constant_dynamic-update-slice_fusion), channel_id=1, source_target_pairs={{0,24},{1,25},{2,26},{3,27},{4,28},{5,29},{6,30},{7,31},{8,32},{9,... | collective-permute-start | bytes 4718600 | tf_op jit(solution)/shard_map/ppermute | solution.py:16
  16.6 3.5 collective-permute-start.3
  20.0 6.3 %collective-permute-start.4 = (bf16[1,1,256,3072]{3,2,1,0:T(8,128)(2,1)S(1)}, bf16[1,1,256,3072]{3,2,1,0:T(8,128)(2,1)}, u32[]{:S(2)}, u32[]{:S(2)}) collective-permute-start(bf16[1,1,256,3072]{3,2,1,0:T(8,128)(2,1)S(1)} %constant_dynamic-update-slice_fusion), channel_id=1, source_target_pairs={{8,0},{9,1},{10,2},{11,3},{12,4},{13,5},{14,6},{15,7},{16,8},{17,9... | collective-permute-start | bytes 4718600 | tf_op jit(solution)/shard_map/ppermute | solution.py:16
  26.3 75.1 %collective-permute-done = bf16[1,1,256,3072]{3,2,1,0:T(8,128)(2,1)S(1)} collective-permute-done((bf16[1,1,256,3072]{3,2,1,0:T(8,128)(2,1)S(1)}, bf16[1,1,256,3072]{3,2,1,0:T(8,128)(2,1)S(1)}, u32[]{:S(2)}, u32[]{:S(2)}) %collective-permute-start) | collective-permute-done | bytes 1572896 | tf_op jit(solution)/shard_map/ppermute | solution.py:16
  101.4 40.7 %collective-permute-start.5 = (bf16[1,1,256,3072]{3,2,1,0:T(8,128)(2,1)S(1)}, bf16[1,1,256,3072]{3,2,1,0:T(8,128)(2,1)}, u32[]{:S(2)}, u32[]{:S(2)}) collective-permute-start(bf16[1,1,256,3072]{3,2,1,0:T(8,128)(2,1)S(1)} %constant_dynamic-update-slice_fusion), channel_id=1, source_target_pairs={{24,0},{25,1},{26,2},{27,3},{28,4},{29,5},{30,6},{31,7},{32,8},{33... | collective-permute-start | bytes 4718600 | tf_op jit(solution)/shard_map/ppermute | solution.py:16
  142.2 38.2 %collective-permute-start.6 = (bf16[1,1,256,3072]{3,2,1,0:T(8,128)(2,1)S(1)}, bf16[1,1,256,3072]{3,2,1,0:T(8,128)(2,1)}, u32[]{:S(2)}, u32[]{:S(2)}) collective-permute-start(bf16[1,1,256,3072]{3,2,1,0:T(8,128)(2,1)S(1)} %constant_dynamic-update-slice_fusion), channel_id=1, source_target_pairs={{32,0},{33,1},{34,2},{35,3},{36,4},{37,5},{38,6},{39,7},{40,8},{41... | collective-permute-start | bytes 4718600 | tf_op jit(solution)/shard_map/ppermute | solution.py:16
  180.4 69.5 %collective-permute-done.2 = bf16[1,1,256,3072]{3,2,1,0:T(8,128)(2,1)S(1)} collective-permute-done((bf16[1,1,256,3072]{3,2,1,0:T(8,128)(2,1)S(1)}, bf16[1,1,256,3072]{3,2,1,0:T(8,128)(2,1)S(1)}, u32[]{:S(2)}, u32[]{:S(2)}) %collective-permute-start.2) | collective-permute-done | bytes 1572896 | tf_op jit(solution)/shard_map/ppermute | solution.py:16
  249.8 9.1 %collective-permute-start.7 = (bf16[1,1,256,3072]{3,2,1,0:T(8,128)(2,1)S(1)}, bf16[1,1,256,3072]{3,2,1,0:T(8,128)(2,1)}, u32[]{:S(2)}, u32[]{:S(2)}) collective-permute-start(bf16[1,1,256,3072]{3,2,1,0:T(8,128)(2,1)S(1)} %constant_dynamic-update-slice_fusion), channel_id=1, source_target_pairs={{40,0},{41,1},{42,2},{43,3},{44,4},{45,5},{46,6},{47,7},{48,8},{49... | collective-permute-start | bytes 4718600 | tf_op jit(solution)/shard_map/ppermute | solution.py:16
  259.0 0.8 copy.7
  259.8 0.6 fusion.12
  260.4 0.8 copy.8
  261.2 154.1 %collective-permute-done.3 = bf16[1,1,256,3072]{3,2,1,0:T(8,128)(2,1)} collective-permute-done((bf16[1,1,256,3072]{3,2,1,0:T(8,128)(2,1)S(1)}, bf16[1,1,256,3072]{3,2,1,0:T(8,128)(2,1)}, u32[]{:S(2)}, u32[]{:S(2)}) %collective-permute-start.3) | collective-permute-done | bytes 1572896 | tf_op jit(solution)/shard_map/ppermute | solution.py:16
  415.3 97.3 %collective-permute-done.4 = bf16[1,1,256,3072]{3,2,1,0:T(8,128)(2,1)} collective-permute-done((bf16[1,1,256,3072]{3,2,1,0:T(8,128)(2,1)S(1)}, bf16[1,1,256,3072]{3,2,1,0:T(8,128)(2,1)}, u32[]{:S(2)}, u32[]{:S(2)}) %collective-permute-start.4) | collective-permute-done | bytes 1572896 | tf_op jit(solution)/shard_map/ppermute | solution.py:16
  512.5 8.0 %collective-permute-done.7 = bf16[1,1,256,3072]{3,2,1,0:T(8,128)(2,1)} collective-permute-done((bf16[1,1,256,3072]{3,2,1,0:T(8,128)(2,1)S(1)}, bf16[1,1,256,3072]{3,2,1,0:T(8,128)(2,1)}, u32[]{:S(2)}, u32[]{:S(2)}) %collective-permute-start.7) | collective-permute-done | bytes 1572896 | tf_op jit(solution)/shard_map/ppermute | solution.py:16
  520.6 10.1 %maximum_maximum_fusion = bf16[3,3,256,3072]{3,2,1,0:T(8,128)(2,1)} fusion(bf16[1,1,256,3072]{3,2,1,0:T(8,128)(2,1)} %collective-permute-done.7, bf16[1,1,256,3072]{3,2,1,0:T(8,128)(2,1)} %collective-permute-done.6, bf16[1,1,256,3072]{3,2,1,0:T(8,128)(2,1)} %collective-permute-done.5, bf16[1,1,256,3072]{3,2,1,0:T(8,128)(2,1)} %collective-permute-done.4, ...), kind=kLoop, calls=%fused_computation.16 | loop fusion | flops 56623104 | bytes 28311552 | tf_op jit(solution)/shard_map/concatenate | solution.py:64
  530.7 57.2 %while.13 = (s32[]{:T(128)}, bf16[12,128,128]{1,2,0:T(8,128)(2,1)S(1)}, s32[12]{0:T(128)S(1)}, bf16[128,1536]{1,0:T(8,128)(2,1)}, bf16[2304,3072]{1,0:T(8,128)(2...) while((s32[]{:T(128)}, ...), condition=%wide.region_3.4_spmd.clone, body=%wide.region_0.3_spmd.clone.sunk | while | flops 153356288 | bytes 4829466 | solution.py:43
  530.7 0.6 dynamic_slice.53
  532.0 1.5 fusion.19
  533.5 0.3 fusion.20
  533.9 1.6 fusion.21
  535.5 0.6 dynamic_slice.53
  536.8 1.5 fusion.19
  538.6 1.6 fusion.21
  540.2 0.6 dynamic_slice.53
  541.6 1.5 fusion.19
  543.1 0.3 fusion.20
  543.4 1.6 fusion.21
  545.0 0.6 dynamic_slice.53
  546.3 1.5 fusion.19
  547.8 0.3 fusion.20
  548.2 1.6 fusion.21
  549.8 0.6 dynamic_slice.53
  551.1 1.5 fusion.19
  552.6 0.3 fusion.20
  552.9 1.6 fusion.21
  554.5 0.6 dynamic_slice.53
  555.9 1.5 fusion.19
  557.7 1.6 fusion.21
  559.3 0.6 dynamic_slice.53
  560.7 1.5 fusion.19
  562.1 0.3 fusion.20
  562.5 1.6 fusion.21
  564.1 0.6 dynamic_slice.53
  565.4 1.5 fusion.19
  567.2 1.6 fusion.21
  568.8 0.6 dynamic_slice.53
  570.2 1.5 fusion.19
  571.7 0.3 fusion.20
  572.0 1.6 fusion.21
  573.6 0.6 dynamic_slice.53
  575.0 1.5 fusion.19
  576.8 1.6 fusion.21
  578.4 0.6 dynamic_slice.53
  579.7 1.5 fusion.19
  581.2 0.3 fusion.20
  581.6 1.6 fusion.21
  583.2 0.6 dynamic_slice.53
  584.5 1.5 fusion.19
  586.0 0.3 fusion.20
  586.3 1.6 fusion.21
  587.9 0.9 copy.10
  (40 shorter events, 2.6 us)
Async XLA Ops:
  0.0 1.4 copy-start.2
  1.5 99.9 %collective-permute-start = (bf16[1,1,256,3072]{3,2,1,0:T(8,128)(2,1)S(1)}, bf16[1,1,256,3072]{3,2,1,0:T(8,128)(2,1)S(1)}, u32[]{:S(2)}, u32[]{:S(2)}) collective-permute-start(bf16[1,1,256,3072]{3,2,1,0:T(8,128)(2,1)S(1)} %constant_dynamic-update-slice_fusion), channel_id=1, source_target_pairs={{0,40},{1,41},{2,42},{3,43},{4,44},{5,45},{6,46},{7,47},{8,48},{9,... | collective-permute-start | bytes 4718600 | tf_op jit(solution)/shard_map/ppermute | solution.py:16
  4.3 137.8 %collective-permute-start.1 = (bf16[1,1,256,3072]{3,2,1,0:T(8,128)(2,1)S(1)}, bf16[1,1,256,3072]{3,2,1,0:T(8,128)(2,1)S(1)}, u32[]{:S(2)}, u32[]{:S(2)}) collective-permute-start(bf16[1,1,256,3072]{3,2,1,0:T(8,128)(2,1)S(1)} %constant_dynamic-update-slice_fusion), channel_id=1, source_target_pairs={{0,32},{1,33},{2,34},{3,35},{4,36},{5,37},{6,38},{7,39},{8,40},{9,... | collective-permute-start | bytes 4718600 | tf_op jit(solution)/shard_map/ppermute | solution.py:16
  7.5 242.4 %collective-permute-start.2 = (bf16[1,1,256,3072]{3,2,1,0:T(8,128)(2,1)S(1)}, bf16[1,1,256,3072]{3,2,1,0:T(8,128)(2,1)S(1)}, u32[]{:S(2)}, u32[]{:S(2)}) collective-permute-start(bf16[1,1,256,3072]{3,2,1,0:T(8,128)(2,1)S(1)} %constant_dynamic-update-slice_fusion), channel_id=1, source_target_pairs={{0,24},{1,25},{2,26},{3,27},{4,28},{5,29},{6,30},{7,31},{8,32},{9,... | collective-permute-start | bytes 4718600 | tf_op jit(solution)/shard_map/ppermute | solution.py:16
  16.6 398.7 %collective-permute-start.3 = (bf16[1,1,256,3072]{3,2,1,0:T(8,128)(2,1)S(1)}, bf16[1,1,256,3072]{3,2,1,0:T(8,128)(2,1)}, u32[]{:S(2)}, u32[]{:S(2)}) collective-permute-start(bf16[1,1,256,3072]{3,2,1,0:T(8,128)(2,1)S(1)} %constant_dynamic-update-slice_fusion), channel_id=1, source_target_pairs={{0,8},{1,9},{2,10},{3,11},{4,12},{5,13},{6,14},{7,15},{8,16},{9,17... | collective-permute-start | bytes 4718600 | tf_op jit(solution)/shard_map/ppermute | solution.py:16
  20.0 492.5 %collective-permute-start.4 = (bf16[1,1,256,3072]{3,2,1,0:T(8,128)(2,1)S(1)}, bf16[1,1,256,3072]{3,2,1,0:T(8,128)(2,1)}, u32[]{:S(2)}, u32[]{:S(2)}) collective-permute-start(bf16[1,1,256,3072]{3,2,1,0:T(8,128)(2,1)S(1)} %constant_dynamic-update-slice_fusion), channel_id=1, source_target_pairs={{8,0},{9,1},{10,2},{11,3},{12,4},{13,5},{14,6},{15,7},{16,8},{17,9... | collective-permute-start | bytes 4718600 | tf_op jit(solution)/shard_map/ppermute | solution.py:16
  101.4 411.2 %collective-permute-start.5 = (bf16[1,1,256,3072]{3,2,1,0:T(8,128)(2,1)S(1)}, bf16[1,1,256,3072]{3,2,1,0:T(8,128)(2,1)}, u32[]{:S(2)}, u32[]{:S(2)}) collective-permute-start(bf16[1,1,256,3072]{3,2,1,0:T(8,128)(2,1)S(1)} %constant_dynamic-update-slice_fusion), channel_id=1, source_target_pairs={{24,0},{25,1},{26,2},{27,3},{28,4},{29,5},{30,6},{31,7},{32,8},{33... | collective-permute-start | bytes 4718600 | tf_op jit(solution)/shard_map/ppermute | solution.py:16
  142.1 107.7 %copy-start = (bf16[1,1,256,3072]{3,2,1,0:T(8,128)(2,1)}, bf16[1,1,256,3072]{3,2,1,0:T(8,128)(2,1)S(1)}, u32[]{:S(2)}) copy-start(bf16[1,1,256,3072]{3,2,1,0:T(8,128)(2,1)S(1)} %collective-permute-done.1) | copy-start | bytes 4718596
  142.2 370.4 %collective-permute-start.6 = (bf16[1,1,256,3072]{3,2,1,0:T(8,128)(2,1)S(1)}, bf16[1,1,256,3072]{3,2,1,0:T(8,128)(2,1)}, u32[]{:S(2)}, u32[]{:S(2)}) collective-permute-start(bf16[1,1,256,3072]{3,2,1,0:T(8,128)(2,1)S(1)} %constant_dynamic-update-slice_fusion), channel_id=1, source_target_pairs={{32,0},{33,1},{34,2},{35,3},{36,4},{37,5},{38,6},{39,7},{40,8},{41... | collective-permute-start | bytes 4718600 | tf_op jit(solution)/shard_map/ppermute | solution.py:16
  249.8 9.1 %copy-start.1 = (bf16[1,1,256,3072]{3,2,1,0:T(8,128)(2,1)}, bf16[1,1,256,3072]{3,2,1,0:T(8,128)(2,1)S(1)}, u32[]{:S(2)}) copy-start(bf16[1,1,256,3072]{3,2,1,0:T(8,128)(2,1)S(1)} %collective-permute-done.2) | copy-start | bytes 4718596
  249.8 270.8 %collective-permute-start.7 = (bf16[1,1,256,3072]{3,2,1,0:T(8,128)(2,1)S(1)}, bf16[1,1,256,3072]{3,2,1,0:T(8,128)(2,1)}, u32[]{:S(2)}, u32[]{:S(2)}) collective-permute-start(bf16[1,1,256,3072]{3,2,1,0:T(8,128)(2,1)S(1)} %constant_dynamic-update-slice_fusion), channel_id=1, source_target_pairs={{40,0},{41,1},{42,2},{43,3},{44,4},{45,5},{46,6},{47,7},{48,8},{49... | collective-permute-start | bytes 4718600 | tf_op jit(solution)/shard_map/ppermute | solution.py:16
where the time goes:
time: 590 us; the launch traced here: 589 us
  waiting for transfers between devices  404 us (68%)
  starting transfers between devices  113 us (19%)
  matrix products  36.7 us (6%)
  other arithmetic  15.5 us (3%)
  local copies, waits for them, and re-layouts  11.2 us (2%)
  loops' own time  8.42 us (1%)
    ppermute x8, waiting for transfers between devices, passed_along(): return lax.ppermute(shard, axis, pairs)  404 us
    ppermute x8, starting transfers between devices, passed_along(): return lax.ppermute(shard, axis, pairs)  113 us
    dot_general x12, matrix products, one_head(): return jnp.dot(weights, value_head, preferred_element_type=jnp.float32)  18.9 us
    dot_general x12, matrix products, one_head(): lax.dot_general(query_head, key_head, (((1,), (1,)), ((), ())), preferred...  17.9 us
  transfers between devices with their start and end apart: 8, of which 5 were waited for; matrix products, arithmetic and copies ran while one was open for 0% of the time, Pallas kernels for 0%

commit v1 on v0

v1 whole, which is shorter than its diff:
```python
import functools

import jax
import jax.numpy as jnp
from jax import lax
from jax.experimental import pallas as pl
from jax.experimental.pallas import tpu as pltpu
from jax.sharding import PartitionSpec as P

HDIM = 128
TILE = 256
QROWS = 128
RT = 4
LOG2E = 1.4426950408889634
DEAD = -1e30
AHEAD = 4
STAT = 16

KV_X, KV_Y, Q_P, Q_X, O_P, O_X = range(6)


def split3(row):
    high = row.astype(jnp.bfloat16).astype(jnp.float32)
    rest = row - high
    middle = rest.astype(jnp.bfloat16).astype(jnp.float32)
    return high, middle, rest - middle


def packed_stats(top, total):
    rows = split3(top) + split3(total)
    at = lax.broadcasted_iota(jnp.int32, (STAT, top.shape[1]), 0)
    out = jnp.zeros((STAT, top.shape[1]), jnp.float32)
    for i, row in enumerate(rows):
        out = jnp.where(at == i, row, out)
    return out.astype(jnp.bfloat16)


def kernel(
    heads, columns, frames, q_hbm, k_hbm, v_hbm, pads, out, kv, qb, part, part_stat,
    to_p, to_x, from_p, from_x, local_sem, send_sem, recv_sem,
):
    scale = HDIM ** (-0.5) * LOG2E
    frame, row = lax.axis_index("frame"), lax.axis_index("row")
    rows = RT * columns
    half = 2 * columns
    even = lax.rem(frame, 2) == 0
    r = row // columns
    inner = jnp.logical_or(r == 1, r == 2)
    other_frame = jnp.where(even, frame + 1, frame - 1)
    far_frame = jnp.where(even, frame - 1, frame + 1)
    ahead_frame = lax.rem(jnp.where(even, frame + 2, frame + frames - 2), frames)
    behind_frame = lax.rem(jnp.where(even, frame + frames - 2, frame + 2), frames)
    p_row = (row // half) * half + lax.rem(lax.rem(row, half) + columns, half)
    x_row = lax.rem(row + half, rows)

    across = (other_frame, row)
    onward = (ahead_frame, row)
    side = (frame, p_row)
    cross = (frame, x_row)

    def local(h):
        cut = pl.ds(pl.multiple_of(h * HDIM, HDIM), HDIM)
        return (
            pltpu.make_async_copy(q_hbm.at[0, 0, :, cut], qb.at[h, pl.ds(0, QROWS)], local_sem.at[0, h]),
            pltpu.make_async_copy(k_hbm.at[0, 0, :, cut], kv.at[0, h, pl.ds(0, TILE)], local_sem.at[1, h]),
            pltpu.make_async_copy(v_hbm.at[0, 0, :, cut], kv.at[0, h, pl.ds(TILE, TILE)], local_sem.at[2, h]),
        )

    def remote(kind, h):
        src, dst, device = {
            KV_X: lambda: (kv.at[0, h], kv.at[1, h], across),
            KV_Y: lambda: (kv.at[1, h], kv.at[2, h], onward),
            Q_P: lambda: (qb.at[h, pl.ds(0, QROWS)], qb.at[h, pl.ds(QROWS, QROWS)], side),
            Q_X: lambda: (qb.at[h, pl.ds(QROWS, QROWS)], qb.at[h, pl.ds(2 * QROWS, QROWS)], cross),
            O_P: lambda: (to_p.at[h], from_p.at[h], side),
            O_X: lambda: (to_x.at[h], from_x.at[h], cross),
        }[kind]()
        return pltpu.make_async_remote_copy(
            src_ref=src, dst_ref=dst, send_sem=send_sem.at[kind, h], recv_sem=recv_sem.at[kind, h],
            device_id=device, device_id_type=pl.DeviceIdType.MESH,
        )

    @pl.loop(0, heads)
    def _(h):
        for copy in local(h):
            copy.start()

    barrier = pltpu.get_barrier_semaphore()
    for device in (across, onward, (behind_frame, row), side, cross):
        pl.semaphore_signal(barrier, inc=1, device_id=device, device_id_type=pl.DeviceIdType.MESH)

    live0 = TILE - pads[frame, row]
    live1 = TILE - pads[other_frame, row]
    far_there = jnp.logical_and(far_frame >= 0, far_frame < frames)
    live2 = jnp.where(far_there, TILE - pads[jnp.clip(far_frame, 0, frames - 1), row], 0)
    lives = (live0, live1, live2)

    pl.semaphore_wait(barrier, 5)

    def send_own(h):
        for copy in local(h):
            copy.wait()
        remote(Q_P, h).start()
        remote(KV_X, h).start()

    def attend(h, queries):
        at = lax.broadcasted_iota(jnp.int32, (TILE, queries.shape[0]), 0)
        scores = []
        for slot in range(3):
            s = lax.dot_general(
                kv[slot, h, 0:TILE], queries, (((1,), (1,)), ((), ())), preferred_element_type=jnp.float32
            )
            scores.append(jnp.where(at < lives[slot], s, DEAD))
        top = functools.reduce(jnp.maximum, [jnp.max(s, axis=0, keepdims=True) for s in scores])
        total, acc = 0.0, 0.0
        for slot in range(3):
            expo = jnp.exp2((scores[slot] - top) * scale)
            total = total + jnp.sum(expo, axis=0, keepdims=True)
            acc = acc + lax.dot_general(
                kv[slot, h, TILE:2 * TILE], expo.astype(jnp.bfloat16), (((0,), (0,)), ((), ())),
                preferred_element_type=jnp.float32,
            )
        return acc, top, total

    def packed_into(ref, h, acc, top, total):
        ref[h, 0:HDIM] = acc.astype(jnp.bfloat16)
        ref[h, HDIM:HDIM + STAT] = packed_stats(top, total)

    def keep(which, h, acc, top, total):
        part[which, h] = acc
        part_stat[which, h, 0:1] = top
        part_stat[which, h, 1:2] = total

    def merged(which, h, ref):
        stats = ref[h, HDIM:HDIM + STAT].astype(jnp.float32)
        top2 = stats[0:1] + stats[1:2] + stats[2:3]
        total2 = stats[3:4] + stats[4:5] + stats[5:6]
        top1, total1 = part_stat[which, h, 0:1], part_stat[which, h, 1:2]
        top = jnp.maximum(top1, top2)
        w1, w2 = jnp.exp2((top1 - top) * scale), jnp.exp2((top2 - top) * scale)
        acc = part[which, h] * w1 + ref[h, 0:HDIM].astype(jnp.float32) * w2
        return acc, top, total1 * w1 + total2 * w2

    @pl.loop(0, min(AHEAD, heads))
    def _(h):
        send_own(h)

    @pl.loop(0, heads + 3)
    def _(t):
        @pl.when(t + AHEAD < heads)
        def _():
            send_own(t + AHEAD)

        @pl.when(t < heads)
        def _():
            remote(Q_P, t).wait_recv()

            @pl.when(jnp.logical_not(inner))
            def _():
                remote(Q_X, t).start()

            remote(KV_X, t).wait_recv()
            remote(KV_Y, t).start()

        @pl.when(jnp.logical_and(t >= 1, t < heads + 1))
        def _():
            h = t - 1
            remote(KV_Y, h).wait_recv()

            @pl.when(inner)
            def _():
                remote(Q_X, h).wait_recv()
                packed_into(to_x, h, *attend(h, qb[h, 2 * QROWS:3 * QROWS]))
                remote(O_X, h).start()

            acc, top, total = attend(h, qb[h, 0:2 * QROWS])
            keep(0, h, acc[:, 0:QROWS], top[:, 0:QROWS], total[:, 0:QROWS])
            for_p = acc[:, QROWS:], top[:, QROWS:], total[:, QROWS:]

            @pl.when(inner)
            def _():
                packed_into(to_p, h, *for_p)
                remote(O_P, h).start()

            @pl.when(jnp.logical_not(inner))
            def _():
                keep(1, h, *for_p)

        @pl.when(jnp.logical_and(jnp.logical_not(inner), jnp.logical_and(t >= 2, t < heads + 2)))
        def _():
            h = t - 2
            remote(O_X, h).wait_recv()
            packed_into(to_p, h, *merged(1, h, from_x))
            remote(O_P, h).start()

        @pl.when(t >= 3)
        def _():
            h = t - 3
            remote(O_P, h).wait_recv()
            acc, top, total = merged(0, h, from_p)
            done = jnp.transpose(acc / total)
            out[0, 0, :, pl.ds(pl.multiple_of(h * HDIM, HDIM), HDIM)] = done.astype(out.dtype)

    @pl.loop(0, heads)
    def _(h):
        for kind in (KV_X, KV_Y, Q_P, O_P):
            remote(kind, h).wait_send()

        @pl.when(inner)
        def _():
            remote(O_X, h).wait_send()

        @pl.when(jnp.logical_not(inner))
        def _():
            remote(Q_X, h).wait_send()


def shards(queries, keys, values, pad_counts):
    width = queries.shape[-1]
    heads = width // HDIM
    frames, rows = pad_counts.shape
    bf16 = jnp.bfloat16
    return pl.pallas_call(
        functools.partial(kernel, heads, rows // RT, frames),
        out_shape=jax.ShapeDtypeStruct(queries.shape, bf16),
        in_specs=[pl.BlockSpec(memory_space=pl.ANY)] * 3 + [pl.BlockSpec(memory_space=pltpu.SMEM)],
        out_specs=pl.BlockSpec(memory_space=pltpu.VMEM),
        scratch_shapes=[
            pltpu.VMEM((3, heads, 2 * TILE, HDIM), bf16),
            pltpu.VMEM((heads, 3 * QROWS, HDIM), bf16),
            pltpu.VMEM((2, heads, HDIM, QROWS), jnp.float32),
            pltpu.VMEM((2, heads, 8, QROWS), jnp.float32),
        ]
        + [pltpu.VMEM((heads, HDIM + STAT, QROWS), bf16)] * 4
        + [
            pltpu.SemaphoreType.DMA((3, heads)),
            pltpu.SemaphoreType.DMA((6, heads)),
            pltpu.SemaphoreType.DMA((6, heads)),
        ],
        compiler_params=pltpu.CompilerParams(
            collective_id=0, has_side_effects=True, vmem_limit_bytes=40 * 1024 * 1024
        ),
    )(queries, keys, values, pad_counts)


def solution(mesh):
    spec = P("frame", "row", None, None)
    return jax.shard_map(
        shards, mesh=mesh, in_specs=(spec, spec, spec, P()), out_specs=spec, check_vma=False
    )
```

time: 590 us -> 89.1 us (0.15)
  the two profiles are of different devices: /device:TPU:392 before, /device:TPU:4 now
where the time goes in v1:
time: 89.1 us; the launch traced here: 88.9 us
  Pallas kernels  84.1 us (94%)
  local copies, waits for them, and re-layouts  4.71 us (5%)
    pallas_call x1, Pallas kernels, shards(): pl.pallas_call(functools.partial(kernel, heads, rows // RT, frames), out_...  84.1 us
    unnamed x9, local copies, waits for them, and re-layouts  4.71 us

profile of v1, /device:TPU:4, one launch (start us, length us, event | category | flops | bytes accessed | tf_op | source)
XLA Modules:
  0.0 88.9 jit_solution(2909350200704119138)
XLA Ops:
  0.0 0.0 copy-start
  0.0 1.1 %copy-done = bf16[1,1,256,1536]{3,2,1,0:T(8,128)(2,1)S(1)} copy-done((bf16[1,1,256,1536]{3,2,1,0:T(8,128)(2,1)S(1)}, bf16[1,1,256,1536]{3,2,1,0:T(8,128)(2,1)}, u32[]{:S(2)}) %copy-start) | copy-done | bytes 786456
  1.1 0.0 copy-start.1
  1.1 1.1 %copy-done.1 = bf16[1,1,256,1536]{3,2,1,0:T(8,128)(2,1)S(1)} copy-done((bf16[1,1,256,1536]{3,2,1,0:T(8,128)(2,1)S(1)}, bf16[1,1,256,1536]{3,2,1,0:T(8,128)(2,1)}, u32[]{:S(2)}) %copy-start.1) | copy-done | bytes 786456
  2.3 0.0 copy-start.2
  2.3 1.0 %copy-done.2 = bf16[1,1,128,1536]{3,2,1,0:T(8,128)(2,1)S(1)} copy-done((bf16[1,1,128,1536]{3,2,1,0:T(8,128)(2,1)S(1)}, bf16[1,1,128,1536]{3,2,1,0:T(8,128)(2,1)}, u32[]{:S(2)}) %copy-start.2) | copy-done | bytes 393240
  3.3 0.0 copy-start.3
  3.3 0.7 copy-done.3
  4.0 84.1 %shard_map.46 = bf16[1,1,128,1536]{3,2,1,0:T(8,128)(2,1)S(1)} custom-call(bf16[1,1,128,1536]{3,2,1,0:T(8,128)(2,1)S(1)} %copy-done.2, bf16[1,1,256,1536]{3,2,1,0:T(8,128)(2,1)S(1)} %copy-done, bf16[1,1,256,1536]{3,2,1,0:T(8,128)(2,1)S(1)} %copy-done.1, s32[16,32]{1,0:T(8,128)S(1)} %copy-done.3), custom_call_target="tpu_custom_call" | custom-call | tf_op jit(solution)/shard_map/pallas_call | solution.py:223
  88.1 0.7 copy.6
Async XLA Ops:
  0.0 1.1 %copy-start = (bf16[1,1,256,1536]{3,2,1,0:T(8,128)(2,1)S(1)}, bf16[1,1,256,1536]{3,2,1,0:T(8,128)(2,1)}, u32[]{:S(2)}) copy-start(bf16[1,1,256,1536]{3,2,1,0:T(8,128)(2,1)} %k_hbm.1) | copy-start | bytes 2359300
  1.1 1.1 %copy-start.1 = (bf16[1,1,256,1536]{3,2,1,0:T(8,128)(2,1)S(1)}, bf16[1,1,256,1536]{3,2,1,0:T(8,128)(2,1)}, u32[]{:S(2)}) copy-start(bf16[1,1,256,1536]{3,2,1,0:T(8,128)(2,1)} %v_hbm.1) | copy-start | bytes 2359300
  2.3 1.0 %copy-start.2 = (bf16[1,1,128,1536]{3,2,1,0:T(8,128)(2,1)S(1)}, bf16[1,1,128,1536]{3,2,1,0:T(8,128)(2,1)}, u32[]{:S(2)}) copy-start(bf16[1,1,128,1536]{3,2,1,0:T(8,128)(2,1)} %q_hbm.1) | copy-start | bytes 1179652
  3.3 0.7 copy-start.3

commit v2 on v1

--- a/solution.py
+++ b/solution.py
@@ -12,8 +12,8 @@
 QROWS = 128
 RT = 4
 LOG2E = 1.4426950408889634
-DEAD = -1e30
 AHEAD = 4
+LAG = 2
 STAT = 16
 
 KV_X, KV_Y, Q_P, Q_X, O_P, O_X = range(6)
@@ -37,7 +37,7 @@
 
 def kernel(
     heads, columns, frames, q_hbm, k_hbm, v_hbm, pads, out, kv, qb, part, part_stat,
-    to_p, to_x, from_p, from_x, local_sem, send_sem, recv_sem,
+    to_p, to_x, from_p, from_x, raw_k, raw_v, live_rows, local_sem, send_sem, recv_sem,
 ):
     scale = HDIM ** (-0.5) * LOG2E
     frame, row = lax.axis_index("frame"), lax.axis_index("row")
@@ -62,8 +62,8 @@
         cut = pl.ds(pl.multiple_of(h * HDIM, HDIM), HDIM)
         return (
             pltpu.make_async_copy(q_hbm.at[0, 0, :, cut], qb.at[h, pl.ds(0, QROWS)], local_sem.at[0, h]),
-            pltpu.make_async_copy(k_hbm.at[0, 0, :, cut], kv.at[0, h, pl.ds(0, TILE)], local_sem.at[1, h]),
-            pltpu.make_async_copy(v_hbm.at[0, 0, :, cut], kv.at[0, h, pl.ds(TILE, TILE)], local_sem.at[2, h]),
+            pltpu.make_async_copy(k_hbm.at[0, 0, :, cut], raw_k.at[h], local_sem.at[1, h]),
+            pltpu.make_async_copy(v_hbm.at[0, 0, :, cut], raw_v.at[h], local_sem.at[2, h]),
         )
 
     def remote(kind, h):
@@ -93,34 +93,43 @@
     live1 = TILE - pads[other_frame, row]
     far_there = jnp.logical_and(far_frame >= 0, far_frame < frames)
     live2 = jnp.where(far_there, TILE - pads[jnp.clip(far_frame, 0, frames - 1), row], 0)
-    lives = (live0, live1, live2)
+    lane = lax.broadcasted_iota(jnp.int32, (STAT, TILE), 1)
+    for slot, live in enumerate((live0, live1, live2)):
+        live_rows[slot] = jnp.where(lane < live, 1.0, 0.0).astype(jnp.bfloat16)
 
     pl.semaphore_wait(barrier, 5)
 
     def send_own(h):
-        for copy in local(h):
-            copy.wait()
+        copies = local(h)
+        copies[0].wait()
         remote(Q_P, h).start()
+        copies[1].wait()
+        copies[2].wait()
+        at = lax.broadcasted_iota(jnp.int32, (TILE, HDIM), 0)
+        keys = raw_k[h].astype(jnp.float32)
+        kv[0, h, 0:TILE] = jnp.where(at < live0, keys, keys[0:1]).astype(jnp.bfloat16)
+        values = jnp.where(at < live0, raw_v[h].astype(jnp.float32), 0.0)
+        for i in range(TILE // HDIM):
+            block = jnp.transpose(values[i * HDIM:(i + 1) * HDIM])
+            kv[0, h, TILE + i * HDIM:TILE + (i + 1) * HDIM] = block.astype(jnp.bfloat16)
         remote(KV_X, h).start()
 
     def attend(h, queries):
-        at = lax.broadcasted_iota(jnp.int32, (TILE, queries.shape[0]), 0)
-        scores = []
-        for slot in range(3):
-            s = lax.dot_general(
+        scores = [
+            lax.dot_general(
                 kv[slot, h, 0:TILE], queries, (((1,), (1,)), ((), ())), preferred_element_type=jnp.float32
             )
-            scores.append(jnp.where(at < lives[slot], s, DEAD))
+            for slot in range(3)
+        ]
         top = functools.reduce(jnp.maximum, [jnp.max(s, axis=0, keepdims=True) for s in scores])
-        total, acc = 0.0, 0.0
-        for slot in range(3):
-            expo = jnp.exp2((scores[slot] - top) * scale)
-            total = total + jnp.sum(expo, axis=0, keepdims=True)
-            acc = acc + lax.dot_general(
-                kv[slot, h, TILE:2 * TILE], expo.astype(jnp.bfloat16), (((0,), (0,)), ((), ())),
-                preferred_element_type=jnp.float32,
-            )
-        return acc, top, total
+        expo = jnp.concatenate([jnp.exp2((s - top) * scale).astype(jnp.bfloat16) for s in scores], axis=0)
+        turned = jnp.concatenate(
+            [kv[slot, h, TILE + i * HDIM:TILE + (i + 1) * HDIM] for slot in range(3) for i in range(TILE // HDIM)],
+            axis=1,
+        )
+        alive = jnp.concatenate([live_rows[slot] for slot in range(3)], axis=1)
+        both = jnp.dot(jnp.concatenate([turned, alive], axis=0), expo, preferred_element_type=jnp.float32)
+        return both[0:HDIM], top, both[HDIM:HDIM + 1]
 
     def packed_into(ref, h, acc, top, total):
         ref[h, 0:HDIM] = acc.astype(jnp.bfloat16)
@@ -145,7 +154,10 @@
     def _(h):
         send_own(h)
 
-    @pl.loop(0, heads + 3)
+    def within(at):
+        return jnp.logical_and(at >= 0, at < heads)
+
+    @pl.loop(0, heads + 3 * LAG)
     def _(t):
         @pl.when(t + AHEAD < heads)
         def _():
@@ -162,10 +174,15 @@
             remote(KV_X, t).wait_recv()
             remote(KV_Y, t).start()
 
-        @pl.when(jnp.logical_and(t >= 1, t < heads + 1))
-        def _():
-            h = t - 1
+        @pl.when(within(t - LAG))
+        def _():
+            h = t - LAG
             remote(KV_Y, h).wait_recv()
+
+            @pl.when(jnp.logical_not(far_there))
+            def _():
+                kv[2, h, 0:TILE] = kv[0, h, 0:TILE]
+                kv[2, h, TILE:2 * TILE] = jnp.zeros((TILE, HDIM), jnp.bfloat16)
 
             @pl.when(inner)
             def _():
@@ -186,16 +203,16 @@
             def _():
                 keep(1, h, *for_p)
 
-        @pl.when(jnp.logical_and(jnp.logical_not(inner), jnp.logical_and(t >= 2, t < heads + 2)))
-        def _():
-            h = t - 2
+        @pl.when(jnp.logical_and(jnp.logical_not(inner), within(t - 2 * LAG)))
+        def _():
+            h = t - 2 * LAG
             remote(O_X, h).wait_recv()
             packed_into(to_p, h, *merged(1, h, from_x))
             remote(O_P, h).start()
 
-        @pl.when(t >= 3)
-        def _():
-            h = t - 3
+        @pl.when(t >= 3 * LAG)
+        def _():
+            h = t - 3 * LAG
             remote(O_P, h).wait_recv()
             acc, top, total = merged(0, h, from_p)
             done = jnp.transpose(acc / total)
@@ -232,13 +249,15 @@
             pltpu.VMEM((2, heads, 8, QROWS), jnp.float32),
         ]
         + [pltpu.VMEM((heads, HDIM + STAT, QROWS), bf16)] * 4
+        + [pltpu.VMEM((heads, TILE, HDIM), bf16)] * 2
         + [
+            pltpu.VMEM((3, STAT, TILE), bf16),
             pltpu.SemaphoreType.DMA((3, heads)),
             pltpu.SemaphoreType.DMA((6, heads)),
             pltpu.SemaphoreType.DMA((6, heads)),
         ],
         compiler_params=pltpu.CompilerParams(
-            collective_id=0, has_side_effects=True, vmem_limit_bytes=40 * 1024 * 1024
+            collective_id=0, has_side_effects=True, vmem_limit_bytes=60 * 1024 * 1024
         ),
     )(queries, keys, values, pad_counts)
 

time: 89.1 us -> 75.5 us (0.85)
  Pallas kernels: 84.1 us -> 73.5 us
  local copies, waits for them, and re-layouts: 4.71 us -> 1.77 us
    pallas_call x1, Pallas kernels: 84.1 us -> 73.5 us  [shards(): pl.pallas_call(functools.partial(kernel, heads, rows // RT, frames), out_...]
    unnamed x9 -> x1, local copies, waits for them, and re-layouts: 4.71 us -> 1.77 us
where the time goes in v2:
time: 75.5 us; the launch traced here: 75.3 us
  Pallas kernels  73.5 us (97%)
  local copies, waits for them, and re-layouts  1.77 us (2%)
    pallas_call x1, Pallas kernels, shards(): pl.pallas_call(functools.partial(kernel, heads, rows // RT, frames), out_...  73.5 us
    unnamed x1, local copies, waits for them, and re-layouts  1.77 us

profile of v2, /device:TPU:4, one launch (start us, length us, event | category | flops | bytes accessed | tf_op | source)
XLA Modules:
  0.0 75.3 jit_solution(13519391096668624579)
XLA Ops:
  0.0 73.5 %shard_map.46 = bf16[1,1,128,1536]{3,2,1,0:T(8,128)(2,1)} custom-call(bf16[1,1,128,1536]{3,2,1,0:T(8,128)(2,1)} %q_hbm.1, bf16[1,1,256,1536]{3,2,1,0:T(8,128)(2,1)} %k_hbm.1, bf16[1,1,256,1536]{3,2,1,0:T(8,128)(2,1)} %v_hbm.1, s32[16,32]{1,0:T(8,128)} %pads.1), custom_call_target="tpu_custom_call" | custom-call | tf_op jit(solution)/shard_map/pallas_call | solution.py:240
  73.5 1.8 %copy.6 = bf16[1,1,128,1536]{3,2,1,0:T(8,128)(2,1)} copy(bf16[1,1,128,1536]{3,2,1,0:T(8,128)(2,1)} %shard_map.46) | data formatting | bytes 786432

commit v3 on v2

--- a/solution.py
+++ b/solution.py
@@ -13,10 +13,11 @@
 RT = 4
 LOG2E = 1.4426950408889634
 AHEAD = 4
+Q_AHEAD = 7
 LAG = 2
 STAT = 16
 
-KV_X, KV_Y, Q_P, Q_X, O_P, O_X = range(6)
+KV_X, KV_Y, Q_1, Q_2, Q_X, O_1, O_2, O_X = range(8)
 
 
 def split3(row):
@@ -37,7 +38,7 @@
 
 def kernel(
     heads, columns, frames, q_hbm, k_hbm, v_hbm, pads, out, kv, qb, part, part_stat,
-    to_p, to_x, from_p, from_x, raw_k, raw_v, live_rows, local_sem, send_sem, recv_sem,
+    to_p, to_x, from_p, from_x, raw_k, raw_v, live_rows, via_o, via_q, local_sem, send_sem, recv_sem,
 ):
     scale = HDIM ** (-0.5) * LOG2E
     frame, row = lax.axis_index("frame"), lax.axis_index("row")
@@ -50,29 +51,40 @@
     far_frame = jnp.where(even, frame - 1, frame + 1)
     ahead_frame = lax.rem(jnp.where(even, frame + 2, frame + frames - 2), frames)
     behind_frame = lax.rem(jnp.where(even, frame + frames - 2, frame + 2), frames)
-    p_row = (row // half) * half + lax.rem(lax.rem(row, half) + columns, half)
+    quarter = columns // 2
+    side_base, side_at = (row // half) * half, lax.rem(row, half)
+    up_row = side_base + lax.rem(side_at + quarter, half)
+    down_row = side_base + lax.rem(side_at + half - quarter, half)
     x_row = lax.rem(row + half, rows)
 
     across = (other_frame, row)
     onward = (ahead_frame, row)
-    side = (frame, p_row)
     cross = (frame, x_row)
 
-    def local(h):
-        cut = pl.ds(pl.multiple_of(h * HDIM, HDIM), HDIM)
+    def midway(h, turn):
+        return (frame, jnp.where(lax.rem(h + turn, 2) == 0, up_row, down_row))
+
+    def cut(h):
+        return pl.ds(pl.multiple_of(h * HDIM, HDIM), HDIM)
+
+    def local_queries(h):
+        return pltpu.make_async_copy(q_hbm.at[0, 0, :, cut(h)], qb.at[h, pl.ds(0, QROWS)], local_sem.at[0, h])
+
+    def local_pairs(h):
         return (
-            pltpu.make_async_copy(q_hbm.at[0, 0, :, cut], qb.at[h, pl.ds(0, QROWS)], local_sem.at[0, h]),
-            pltpu.make_async_copy(k_hbm.at[0, 0, :, cut], raw_k.at[h], local_sem.at[1, h]),
-            pltpu.make_async_copy(v_hbm.at[0, 0, :, cut], raw_v.at[h], local_sem.at[2, h]),
+            pltpu.make_async_copy(k_hbm.at[0, 0, :, cut(h)], raw_k.at[h], local_sem.at[1, h]),
+            pltpu.make_async_copy(v_hbm.at[0, 0, :, cut(h)], raw_v.at[h], local_sem.at[2, h]),
         )
 
     def remote(kind, h):
         src, dst, device = {
             KV_X: lambda: (kv.at[0, h], kv.at[1, h], across),
             KV_Y: lambda: (kv.at[1, h], kv.at[2, h], onward),
-            Q_P: lambda: (qb.at[h, pl.ds(0, QROWS)], qb.at[h, pl.ds(QROWS, QROWS)], side),
+            Q_1: lambda: (qb.at[h, pl.ds(0, QROWS)], via_q.at[h], midway(h, 0)),
+            Q_2: lambda: (via_q.at[h], qb.at[h, pl.ds(QROWS, QROWS)], midway(h, 0)),
             Q_X: lambda: (qb.at[h, pl.ds(QROWS, QROWS)], qb.at[h, pl.ds(2 * QROWS, QROWS)], cross),
-            O_P: lambda: (to_p.at[h], from_p.at[h], side),
+            O_1: lambda: (to_p.at[h], via_o.at[h], midway(h, 1)),
+            O_2: lambda: (via_o.at[h], from_p.at[h], midway(h, 1)),
             O_X: lambda: (to_x.at[h], from_x.at[h], cross),
         }[kind]()
         return pltpu.make_async_remote_copy(
@@ -80,14 +92,14 @@
             device_id=device, device_id_type=pl.DeviceIdType.MESH,
         )
 
+    barrier = pltpu.get_barrier_semaphore()
+    for device in (across, onward, (behind_frame, row), (frame, up_row), (frame, down_row), cross):
+        pl.semaphore_signal(barrier, inc=1, device_id=device, device_id_type=pl.DeviceIdType.MESH)
+
     @pl.loop(0, heads)
     def _(h):
-        for copy in local(h):
+        for copy in (*local_pairs(h), local_queries(h)):
             copy.start()
-
-    barrier = pltpu.get_barrier_semaphore()
-    for device in (across, onward, (behind_frame, row), side, cross):
-        pl.semaphore_signal(barrier, inc=1, device_id=device, device_id_type=pl.DeviceIdType.MESH)
 
     live0 = TILE - pads[frame, row]
     live1 = TILE - pads[other_frame, row]
@@ -97,14 +109,13 @@
     for slot, live in enumerate((live0, live1, live2)):
         live_rows[slot] = jnp.where(lane < live, 1.0, 0.0).astype(jnp.bfloat16)
 
-    pl.semaphore_wait(barrier, 5)
-
-    def send_own(h):
-        copies = local(h)
-        copies[0].wait()
-        remote(Q_P, h).start()
-        copies[1].wait()
-        copies[2].wait()
+    def send_queries(h):
+        local_queries(h).wait()
+        remote(Q_1, h).start()
+
+    def prepare(h):
+        for copy in local_pairs(h):
+            copy.wait()
         at = lax.broadcasted_iota(jnp.int32, (TILE, HDIM), 0)
         keys = raw_k[h].astype(jnp.float32)
         kv[0, h, 0:TILE] = jnp.where(at < live0, keys, keys[0:1]).astype(jnp.bfloat16)
@@ -112,7 +123,6 @@
         for i in range(TILE // HDIM):
             block = jnp.transpose(values[i * HDIM:(i + 1) * HDIM])
             kv[0, h, TILE + i * HDIM:TILE + (i + 1) * HDIM] = block.astype(jnp.bfloat16)
-        remote(KV_X, h).start()
 
     def attend(h, queries):
         scores = [
@@ -150,29 +160,70 @@
         acc = part[which, h] * w1 + ref[h, 0:HDIM].astype(jnp.float32) * w2
         return acc, top, total1 * w1 + total2 * w2
 
-    @pl.loop(0, min(AHEAD, heads))
-    def _(h):
-        send_own(h)
+    early, early_queries = min(AHEAD, heads), min(Q_AHEAD, heads)
+
+    @pl.loop(0, early)
+    def _(h):
+        prepare(h)
+
+    pl.semaphore_wait(barrier, 6)
+
+    @pl.loop(0, early_queries)
+    def _(h):
+        send_queries(h)
+
+        @pl.when(h < early)
+        def _():
+            remote(KV_X, h).start()
 
     def within(at):
         return jnp.logical_and(at >= 0, at < heads)
 
-    @pl.loop(0, heads + 3 * LAG)
+    def relay_queries(h):
+        remote(Q_1, h).wait_recv()
+        remote(Q_2, h).start()
+
+    @pl.loop(0, min(3, heads))
+    def _(h):
+        relay_queries(h)
+
+    def side_queries(h):
+        remote(Q_2, h).wait_recv()
+
+        @pl.when(jnp.logical_not(inner))
+        def _():
+            remote(Q_X, h).start()
+
+    side_queries(0)
+
+    @pl.loop(0, heads + 4 * LAG)
     def _(t):
-        @pl.when(t + AHEAD < heads)
-        def _():
-            send_own(t + AHEAD)
-
-        @pl.when(t < heads)
-        def _():
-            remote(Q_P, t).wait_recv()
-
-            @pl.when(jnp.logical_not(inner))
-            def _():
-                remote(Q_X, t).start()
-
+        @pl.when(within(t))
+        def _():
             remote(KV_X, t).wait_recv()
             remote(KV_Y, t).start()
+
+        @pl.when(t + Q_AHEAD < heads)
+        def _():
+            send_queries(t + Q_AHEAD)
+
+        @pl.when(t + AHEAD < heads)
+        def _():
+            prepare(t + AHEAD)
+            remote(KV_X, t + AHEAD).start()
+
+        @pl.when(t + 3 < heads)
+        def _():
+            relay_queries(t + 3)
+
+        @pl.when(t + 1 < heads)
+        def _():
+            side_queries(t + 1)
+
+        @pl.when(within(t - 3 * LAG))
+        def _():
+            remote(O_1, t - 3 * LAG).wait_recv()
+            remote(O_2, t - 3 * LAG).start()
 
         @pl.when(within(t - LAG))
         def _():
@@ -197,7 +248,7 @@
             @pl.when(inner)
             def _():
                 packed_into(to_p, h, *for_p)
-                remote(O_P, h).start()
+                remote(O_1, h).start()
 
             @pl.when(jnp.logical_not(inner))
             def _():
@@ -208,19 +259,19 @@
             h = t - 2 * LAG
             remote(O_X, h).wait_recv()
             packed_into(to_p, h, *merged(1, h, from_x))
-            remote(O_P, h).start()
-
-        @pl.when(t >= 3 * LAG)
-        def _():
-            h = t - 3 * LAG
-            remote(O_P, h).wait_recv()
+            remote(O_1, h).start()
+
+        @pl.when(t >= 4 * LAG)
+        def _():
+            h = t - 4 * LAG
+            remote(O_2, h).wait_recv()
             acc, top, total = merged(0, h, from_p)
             done = jnp.transpose(acc / total)
             out[0, 0, :, pl.ds(pl.multiple_of(h * HDIM, HDIM), HDIM)] = done.astype(out.dtype)
 
     @pl.loop(0, heads)
     def _(h):
-        for kind in (KV_X, KV_Y, Q_P, O_P):
+        for kind in (KV_X, KV_Y, Q_1, Q_2, O_1, O_2):
             remote(kind, h).wait_send()
 
         @pl.when(inner)
@@ -252,9 +303,11 @@
         + [pltpu.VMEM((heads, TILE, HDIM), bf16)] * 2
         + [
             pltpu.VMEM((3, STAT, TILE), bf16),
+            pltpu.VMEM((heads, HDIM + STAT, QROWS), bf16),
+            pltpu.VMEM((heads, QROWS, HDIM), bf16),
             pltpu.SemaphoreType.DMA((3, heads)),
-            pltpu.SemaphoreType.DMA((6, heads)),
-            pltpu.SemaphoreType.DMA((6, heads)),
+            pltpu.SemaphoreType.DMA((8, heads)),
+            pltpu.SemaphoreType.DMA((8, heads)),
         ],
         compiler_params=pltpu.CompilerParams(
             collective_id=0, has_side_effects=True, vmem_limit_bytes=60 * 1024 * 1024

time: 75.5 us -> 78.4 us (1.038)
  the two profiles are of different devices: /device:TPU:4 before, /device:TPU:94 now
where the time goes in v3:
time: 78.4 us; the launch traced here: 78.2 us
  Pallas kernels  76.4 us (97%)
  local copies, waits for them, and re-layouts  1.77 us (2%)
    pallas_call x1, Pallas kernels, shards(): pl.pallas_call(functools.partial(kernel, heads, rows // RT, frames), out_...  76.4 us
    unnamed x1, local copies, waits for them, and re-layouts  1.77 us

profile of v3, /device:TPU:94, one launch (start us, length us, event | category | flops | bytes accessed | tf_op | source)
XLA Modules:
  0.0 78.2 jit_solution(15868189159600556680)
XLA Ops:
  0.0 76.4 %shard_map.46 = bf16[1,1,128,1536]{3,2,1,0:T(8,128)(2,1)} custom-call(bf16[1,1,128,1536]{3,2,1,0:T(8,128)(2,1)} %q_hbm.1, bf16[1,1,256,1536]{3,2,1,0:T(8,128)(2,1)} %k_hbm.1, bf16[1,1,256,1536]{3,2,1,0:T(8,128)(2,1)} %v_hbm.1, s32[16,32]{1,0:T(8,128)} %pads.1), custom_call_target="tpu_custom_call" | custom-call | tf_op jit(solution)/shard_map/pallas_call | solution.py:291
  76.4 1.8 %copy.6 = bf16[1,1,128,1536]{3,2,1,0:T(8,128)(2,1)} copy(bf16[1,1,128,1536]{3,2,1,0:T(8,128)(2,1)} %shard_map.46) | data formatting | bytes 786432

commit v4 on v2

--- a/solution.py
+++ b/solution.py
@@ -36,7 +36,7 @@
 
 
 def kernel(
-    heads, columns, frames, q_hbm, k_hbm, v_hbm, pads, out, kv, qb, part, part_stat,
+    heads, columns, frames, group, q_hbm, k_hbm, v_hbm, pads, out, kv, q_own, q_p, q_x, part, part_stat,
     to_p, to_x, from_p, from_x, raw_k, raw_v, live_rows, local_sem, send_sem, recv_sem,
 ):
     scale = HDIM ** (-0.5) * LOG2E
@@ -58,36 +58,38 @@
     side = (frame, p_row)
     cross = (frame, x_row)
 
-    def local(h):
-        cut = pl.ds(pl.multiple_of(h * HDIM, HDIM), HDIM)
-        return (
-            pltpu.make_async_copy(q_hbm.at[0, 0, :, cut], qb.at[h, pl.ds(0, QROWS)], local_sem.at[0, h]),
-            pltpu.make_async_copy(k_hbm.at[0, 0, :, cut], raw_k.at[h], local_sem.at[1, h]),
-            pltpu.make_async_copy(v_hbm.at[0, 0, :, cut], raw_v.at[h], local_sem.at[2, h]),
-        )
-
-    def remote(kind, h):
-        src, dst, device = {
-            KV_X: lambda: (kv.at[0, h], kv.at[1, h], across),
-            KV_Y: lambda: (kv.at[1, h], kv.at[2, h], onward),
-            Q_P: lambda: (qb.at[h, pl.ds(0, QROWS)], qb.at[h, pl.ds(QROWS, QROWS)], side),
-            Q_X: lambda: (qb.at[h, pl.ds(QROWS, QROWS)], qb.at[h, pl.ds(2 * QROWS, QROWS)], cross),
-            O_P: lambda: (to_p.at[h], from_p.at[h], side),
-            O_X: lambda: (to_x.at[h], from_x.at[h], cross),
-        }[kind]()
-        return pltpu.make_async_remote_copy(
-            src_ref=src, dst_ref=dst, send_sem=send_sem.at[kind, h], recv_sem=recv_sem.at[kind, h],
-            device_id=device, device_id_type=pl.DeviceIdType.MESH,
-        )
-
-    @pl.loop(0, heads)
-    def _(h):
-        for copy in local(h):
-            copy.start()
-
     barrier = pltpu.get_barrier_semaphore()
     for device in (across, onward, (behind_frame, row), side, cross):
         pl.semaphore_signal(barrier, inc=1, device_id=device, device_id_type=pl.DeviceIdType.MESH)
+
+    local = (
+        pltpu.make_async_copy(k_hbm.at[0, 0], raw_k, local_sem.at[0]),
+        pltpu.make_async_copy(v_hbm.at[0, 0], raw_v, local_sem.at[1]),
+        pltpu.make_async_copy(q_hbm.at[0, 0], q_own, local_sem.at[2]),
+    )
+    for copy in local:
+        copy.start()
+
+    def cut(h, count=1):
+        return pl.ds(pl.multiple_of(h * HDIM, HDIM), count * HDIM)
+
+    def remote(kind, at=None):
+        src, dst, device = {
+            KV_X: (kv.at[0], kv.at[1], across),
+            KV_Y: (kv.at[1], kv.at[2], onward),
+            Q_P: (q_own, q_p, side),
+            Q_X: (q_p, q_x, cross),
+            O_P: (to_p, from_p, side),
+            O_X: (to_x, from_x, cross),
+        }[kind]
+        if at is not None:
+            index = (slice(None), cut(at * group, group)) if kind in (Q_P, Q_X) else (at,)
+            src, dst = src.at[index], dst.at[index]
+        return pltpu.make_async_remote_copy(
+            src_ref=src, dst_ref=dst, send_sem=send_sem.at[kind],
+            recv_sem=recv_sem.at[kind, 0 if at is None else at],
+            device_id=device, device_id_type=pl.DeviceIdType.MESH,
+        )
 
     live0 = TILE - pads[frame, row]
     live1 = TILE - pads[other_frame, row]
@@ -97,22 +99,14 @@
     for slot, live in enumerate((live0, live1, live2)):
         live_rows[slot] = jnp.where(lane < live, 1.0, 0.0).astype(jnp.bfloat16)
 
-    pl.semaphore_wait(barrier, 5)
-
-    def send_own(h):
-        copies = local(h)
-        copies[0].wait()
-        remote(Q_P, h).start()
-        copies[1].wait()
-        copies[2].wait()
+    def prepare(h):
         at = lax.broadcasted_iota(jnp.int32, (TILE, HDIM), 0)
-        keys = raw_k[h].astype(jnp.float32)
+        keys = raw_k[:, cut(h)].astype(jnp.float32)
         kv[0, h, 0:TILE] = jnp.where(at < live0, keys, keys[0:1]).astype(jnp.bfloat16)
-        values = jnp.where(at < live0, raw_v[h].astype(jnp.float32), 0.0)
+        values = jnp.where(at < live0, raw_v[:, cut(h)].astype(jnp.float32), 0.0)
         for i in range(TILE // HDIM):
             block = jnp.transpose(values[i * HDIM:(i + 1) * HDIM])
             kv[0, h, TILE + i * HDIM:TILE + (i + 1) * HDIM] = block.astype(jnp.bfloat16)
-        remote(KV_X, h).start()
 
     def attend(h, queries):
         scores = [
@@ -150,30 +144,61 @@
         acc = part[which, h] * w1 + ref[h, 0:HDIM].astype(jnp.float32) * w2
         return acc, top, total1 * w1 + total2 * w2
 
-    @pl.loop(0, min(AHEAD, heads))
+    early, groups = min(AHEAD, heads), heads // group
+    for copy in local:
+        copy.wait()
+
+    @pl.loop(0, early)
     def _(h):
-        send_own(h)
+        prepare(h)
+
+    pl.semaphore_wait(barrier, 5)
+
+    for g in range(min(2, groups)):
+        remote(Q_P, g).start()
+
+    @pl.loop(0, early)
+    def _(h):
+        remote(KV_X, h).start()
+
+    @pl.loop(early, heads)
+    def _(h):
+        prepare(h)
+
+    def side_queries(g):
+        remote(Q_P, g).wait_recv()
+
+        @pl.when(jnp.logical_not(inner))
+        def _():
+            remote(Q_X, g).start()
+
+    side_queries(0)
 
     def within(at):
         return jnp.logical_and(at >= 0, at < heads)
 
     @pl.loop(0, heads + 3 * LAG)
     def _(t):
-        @pl.when(t + AHEAD < heads)
-        def _():
-            send_own(t + AHEAD)
-
-        @pl.when(t < heads)
-        def _():
-            remote(Q_P, t).wait_recv()
-
-            @pl.when(jnp.logical_not(inner))
-            def _():
-                remote(Q_X, t).start()
-
+        @pl.when(within(t))
+        def _():
             remote(KV_X, t).wait_recv()
             remote(KV_Y, t).start()
 
+        @pl.when(t + AHEAD < heads)
+        def _():
+            remote(KV_X, t + AHEAD).start()
+
+        g = t // group
+        fresh = t == g * group
+
+        @pl.when(jnp.logical_and(fresh, g + 2 < groups))
+        def _():
+            remote(Q_P, g + 2).start()
+
+        @pl.when(jnp.logical_and(fresh, g + 1 < groups))
+        def _():
+            side_queries(g + 1)
+
         @pl.when(within(t - LAG))
         def _():
             h = t - LAG
@@ -186,11 +211,14 @@
 
             @pl.when(inner)
             def _():
-                remote(Q_X, h).wait_recv()
-                packed_into(to_x, h, *attend(h, qb[h, 2 * QROWS:3 * QROWS]))
+                @pl.when(h == (h // group) * group)
+                def _():
+                    remote(Q_X, h // group).wait_recv()
+
+                packed_into(to_x, h, *attend(h, q_x[:, cut(h)]))
                 remote(O_X, h).start()
 
-            acc, top, total = attend(h, qb[h, 0:2 * QROWS])
+            acc, top, total = attend(h, jnp.concatenate([q_own[:, cut(h)], q_p[:, cut(h)]], axis=0))
             keep(0, h, acc[:, 0:QROWS], top[:, 0:QROWS], total[:, 0:QROWS])
             for_p = acc[:, QROWS:], top[:, QROWS:], total[:, QROWS:]
 
@@ -216,44 +244,45 @@
             remote(O_P, h).wait_recv()
             acc, top, total = merged(0, h, from_p)
             done = jnp.transpose(acc / total)
-            out[0, 0, :, pl.ds(pl.multiple_of(h * HDIM, HDIM), HDIM)] = done.astype(out.dtype)
-
-    @pl.loop(0, heads)
-    def _(h):
-        for kind in (KV_X, KV_Y, Q_P, O_P):
-            remote(kind, h).wait_send()
-
-        @pl.when(inner)
-        def _():
-            remote(O_X, h).wait_send()
-
-        @pl.when(jnp.logical_not(inner))
-        def _():
-            remote(Q_X, h).wait_send()
+            out[0, 0, :, cut(h)] = done.astype(out.dtype)
+
+    for kind in (KV_X, KV_Y, Q_P, O_P):
+        remote(kind).wait_send()
+
+    @pl.when(inner)
+    def _():
+        remote(O_X).wait_send()
+
+    @pl.when(jnp.logical_not(inner))
+    def _():
+        remote(Q_X).wait_send()
 
 
 def shards(queries, keys, values, pad_counts):
     width = queries.shape[-1]
     heads = width // HDIM
     frames, rows = pad_counts.shape
+    group = 3 if heads % 3 == 0 else 1
     bf16 = jnp.bfloat16
     return pl.pallas_call(
-        functools.partial(kernel, heads, rows // RT, frames),
+        functools.partial(kernel, heads, rows // RT, frames, group),
         out_shape=jax.ShapeDtypeStruct(queries.shape, bf16),
         in_specs=[pl.BlockSpec(memory_space=pl.ANY)] * 3 + [pl.BlockSpec(memory_space=pltpu.SMEM)],
         out_specs=pl.BlockSpec(memory_space=pltpu.VMEM),
         scratch_shapes=[
             pltpu.VMEM((3, heads, 2 * TILE, HDIM), bf16),
-            pltpu.VMEM((heads, 3 * QROWS, HDIM), bf16),
+            pltpu.VMEM((QROWS, width), bf16),
+            pltpu.VMEM((QROWS, width), bf16),
+            pltpu.VMEM((QROWS, width), bf16),
             pltpu.VMEM((2, heads, HDIM, QROWS), jnp.float32),
             pltpu.VMEM((2, heads, 8, QROWS), jnp.float32),
         ]
         + [pltpu.VMEM((heads, HDIM + STAT, QROWS), bf16)] * 4
-        + [pltpu.VMEM((heads, TILE, HDIM), bf16)] * 2
+        + [pltpu.VMEM((TILE, width), bf16)] * 2
         + [
             pltpu.VMEM((3, STAT, TILE), bf16),
-            pltpu.SemaphoreType.DMA((3, heads)),
-            pltpu.SemaphoreType.DMA((6, heads)),
+            pltpu.SemaphoreType.DMA((3,)),
+            pltpu.SemaphoreType.DMA((6,)),
             pltpu.SemaphoreType.DMA((6, heads)),
         ],
         compiler_params=pltpu.CompilerParams(

time: 75.5 us -> 73 us (0.967)
  Pallas kernels: 73.5 us -> 71 us
    pallas_call x1, Pallas kernels: 73.5 us -> 71 us  [shards(): pl.pallas_call(functools.partial(kernel, heads, rows // RT, frames, group...]
where the time goes in v4:
time: 73 us; the launch traced here: 72.7 us
  Pallas kernels  71 us (97%)
  local copies, waits for them, and re-layouts  1.77 us (2%)
    pallas_call x1, Pallas kernels, shards(): pl.pallas_call(functools.partial(kernel, heads, rows // RT, frames, group...  71 us
    unnamed x1, local copies, waits for them, and re-layouts  1.77 us

profile of v4, /device:TPU:4, one launch (start us, length us, event | category | flops | bytes accessed | tf_op | source)
XLA Modules:
  0.0 72.7 jit_solution(18264932664573193483)
XLA Ops:
  0.0 71.0 %shard_map.46 = bf16[1,1,128,1536]{3,2,1,0:T(8,128)(2,1)} custom-call(bf16[1,1,128,1536]{3,2,1,0:T(8,128)(2,1)} %q_hbm.1, bf16[1,1,256,1536]{3,2,1,0:T(8,128)(2,1)} %k_hbm.1, bf16[1,1,256,1536]{3,2,1,0:T(8,128)(2,1)} %v_hbm.1, s32[16,32]{1,0:T(8,128)} %pads.1), custom_call_target="tpu_custom_call" | custom-call | tf_op jit(solution)/shard_map/pallas_call | solution.py:267
  71.0 1.8 %copy.6 = bf16[1,1,128,1536]{3,2,1,0:T(8,128)(2,1)} copy(bf16[1,1,128,1536]{3,2,1,0:T(8,128)(2,1)} %shard_map.46) | data formatting | bytes 786432

commit v5 on v4

--- a/solution.py
+++ b/solution.py
@@ -12,8 +12,8 @@
 QROWS = 128
 RT = 4
 LOG2E = 1.4426950408889634
-AHEAD = 4
-LAG = 2
+AHEAD = 3
+LAG = 3
 STAT = 16
 
 KV_X, KV_Y, Q_P, Q_X, O_P, O_X = range(6)
@@ -62,12 +62,16 @@
     for device in (across, onward, (behind_frame, row), side, cross):
         pl.semaphore_signal(barrier, inc=1, device_id=device, device_id_type=pl.DeviceIdType.MESH)
 
-    local = (
-        pltpu.make_async_copy(k_hbm.at[0, 0], raw_k, local_sem.at[0]),
-        pltpu.make_async_copy(v_hbm.at[0, 0], raw_v, local_sem.at[1]),
-        pltpu.make_async_copy(q_hbm.at[0, 0], q_own, local_sem.at[2]),
-    )
-    for copy in local:
+    def local(first, count, part_at):
+        span = pl.ds(first * HDIM, count * HDIM)
+        pairs = ((q_hbm, q_own), (k_hbm, raw_k), (v_hbm, raw_v))
+        return [
+            pltpu.make_async_copy(src.at[0, 0, :, span], dst.at[:, span], local_sem.at[part_at, i])
+            for i, (src, dst) in enumerate(pairs)
+        ]
+
+    local_first, local_rest = local(0, group, 0), local(group, heads - group, 1)
+    for copy in local_first + local_rest:
         copy.start()
 
     def cut(h, count=1):
@@ -144,26 +148,29 @@
         acc = part[which, h] * w1 + ref[h, 0:HDIM].astype(jnp.float32) * w2
         return acc, top, total1 * w1 + total2 * w2
 
-    early, groups = min(AHEAD, heads), heads // group
-    for copy in local:
+    early, groups = min(AHEAD, group), heads // group
+    pl.semaphore_wait(barrier, 5)
+    local_first[0].wait()
+    remote(Q_P, 0).start()
+    for copy in local_first[1:]:
         copy.wait()
 
     @pl.loop(0, early)
     def _(h):
         prepare(h)
-
-    pl.semaphore_wait(barrier, 5)
-
-    for g in range(min(2, groups)):
+        remote(KV_X, h).start()
+
+    for copy in local_rest:
+        copy.wait()
+    for g in range(1, min(2, groups)):
         remote(Q_P, g).start()
-
-    @pl.loop(0, early)
-    def _(h):
-        remote(KV_X, h).start()
 
     @pl.loop(early, heads)
     def _(h):
         prepare(h)
+
+    for h in range(early, min(AHEAD, heads)):
+        remote(KV_X, h).start()
 
     def side_queries(g):
         remote(Q_P, g).wait_recv()
@@ -281,7 +288,7 @@
         + [pltpu.VMEM((TILE, width), bf16)] * 2
         + [
             pltpu.VMEM((3, STAT, TILE), bf16),
-            pltpu.SemaphoreType.DMA((3,)),
+            pltpu.SemaphoreType.DMA((2, 3)),
             pltpu.SemaphoreType.DMA((6,)),
             pltpu.SemaphoreType.DMA((6, heads)),
         ],

time: 73 us -> 73.5 us (level)
  the two profiles are of different devices: /device:TPU:4 before, /device:TPU:132 now
where the time goes in v5:
time: 73.5 us; the launch traced here: 73.3 us
  Pallas kernels  71.5 us (97%)
  local copies, waits for them, and re-layouts  1.77 us (2%)
    pallas_call x1, Pallas kernels, shards(): pl.pallas_call(functools.partial(kernel, heads, rows // RT, frames, group...  71.5 us
    unnamed x1, local copies, waits for them, and re-layouts  1.77 us

profile of v5, /device:TPU:132, one launch (start us, length us, event | category | flops | bytes accessed | tf_op | source)
XLA Modules:
  0.0 73.3 jit_solution(16914648458393006770)
XLA Ops:
  0.0 71.5 %shard_map.46 = bf16[1,1,128,1536]{3,2,1,0:T(8,128)(2,1)} custom-call(bf16[1,1,128,1536]{3,2,1,0:T(8,128)(2,1)} %q_hbm.1, bf16[1,1,256,1536]{3,2,1,0:T(8,128)(2,1)} %k_hbm.1, bf16[1,1,256,1536]{3,2,1,0:T(8,128)(2,1)} %v_hbm.1, s32[16,32]{1,0:T(8,128)} %pads.1), custom_call_target="tpu_custom_call" | custom-call | tf_op jit(solution)/shard_map/pallas_call | solution.py:274
  71.6 1.8 %copy.6 = bf16[1,1,128,1536]{3,2,1,0:T(8,128)(2,1)} copy(bf16[1,1,128,1536]{3,2,1,0:T(8,128)(2,1)} %shard_map.46) | data formatting | bytes 786432

commit v6 on v5

--- a/solution.py
+++ b/solution.py
@@ -12,11 +12,11 @@
 QROWS = 128
 RT = 4
 LOG2E = 1.4426950408889634
-AHEAD = 3
-LAG = 3
+AHEAD = 4
+LAG = 2
 STAT = 16
 
-KV_X, KV_Y, Q_P, Q_X, O_P, O_X = range(6)
+KV_X, KV_Y, Q_P, Q_D, Q_B, Q_C, O_P, O_X, O_Y = range(9)
 
 
 def split3(row):
@@ -36,8 +36,8 @@
 
 
 def kernel(
-    heads, columns, frames, group, q_hbm, k_hbm, v_hbm, pads, out, kv, q_own, q_p, q_x, part, part_stat,
-    to_p, to_x, from_p, from_x, raw_k, raw_v, live_rows, local_sem, send_sem, recv_sem,
+    heads, columns, frames, group, q_hbm, k_hbm, v_hbm, pads, out, kv, q_own, q_p, q_a, q_b, q_via, part, part_stat,
+    to_p, to_x, to_y, from_p, from_x, from_y, raw_k, raw_v, live_rows, local_sem, send_sem, recv_sem,
 ):
     scale = HDIM ** (-0.5) * LOG2E
     frame, row = lax.axis_index("frame"), lax.axis_index("row")
@@ -56,10 +56,11 @@
     across = (other_frame, row)
     onward = (ahead_frame, row)
     side = (frame, p_row)
-    cross = (frame, x_row)
+    behind = (behind_frame, row)
+    diagonal = (other_frame, x_row)
 
     barrier = pltpu.get_barrier_semaphore()
-    for device in (across, onward, (behind_frame, row), side, cross):
+    for device in (across, onward, behind, side, diagonal):
         pl.semaphore_signal(barrier, inc=1, device_id=device, device_id_type=pl.DeviceIdType.MESH)
 
     def local(first, count, part_at):
@@ -82,12 +83,15 @@
             KV_X: (kv.at[0], kv.at[1], across),
             KV_Y: (kv.at[1], kv.at[2], onward),
             Q_P: (q_own, q_p, side),
-            Q_X: (q_p, q_x, cross),
+            Q_D: (q_p, q_a, diagonal),
+            Q_B: (q_p, q_via, behind),
+            Q_C: (q_via, q_b, diagonal),
             O_P: (to_p, from_p, side),
-            O_X: (to_x, from_x, cross),
+            O_X: (to_x, from_x, diagonal),
+            O_Y: (to_y, from_y, behind),
         }[kind]
         if at is not None:
-            index = (slice(None), cut(at * group, group)) if kind in (Q_P, Q_X) else (at,)
+            index = (slice(None), cut(at * group, group)) if kind in (Q_P, Q_D, Q_B, Q_C) else (at,)
             src, dst = src.at[index], dst.at[index]
         return pltpu.make_async_remote_copy(
             src_ref=src, dst_ref=dst, send_sem=send_sem.at[kind],
@@ -99,6 +103,8 @@
     live1 = TILE - pads[other_frame, row]
     far_there = jnp.logical_and(far_frame >= 0, far_frame < frames)
     live2 = jnp.where(far_there, TILE - pads[jnp.clip(far_frame, 0, frames - 1), row], 0)
+    third_frame = jnp.where(even, frame + 2, frame - 2)
+    third_there = jnp.logical_and(third_frame >= 0, third_frame < frames)
     lane = lax.broadcasted_iota(jnp.int32, (STAT, TILE), 1)
     for slot, live in enumerate((live0, live1, live2)):
         live_rows[slot] = jnp.where(lane < live, 1.0, 0.0).astype(jnp.bfloat16)
@@ -112,20 +118,20 @@
             block = jnp.transpose(values[i * HDIM:(i + 1) * HDIM])
             kv[0, h, TILE + i * HDIM:TILE + (i + 1) * HDIM] = block.astype(jnp.bfloat16)
 
-    def attend(h, queries):
+    def attend(h, queries, slots):
         scores = [
             lax.dot_general(
                 kv[slot, h, 0:TILE], queries, (((1,), (1,)), ((), ())), preferred_element_type=jnp.float32
             )
-            for slot in range(3)
+            for slot in slots
         ]
         top = functools.reduce(jnp.maximum, [jnp.max(s, axis=0, keepdims=True) for s in scores])
         expo = jnp.concatenate([jnp.exp2((s - top) * scale).astype(jnp.bfloat16) for s in scores], axis=0)
         turned = jnp.concatenate(
-            [kv[slot, h, TILE + i * HDIM:TILE + (i + 1) * HDIM] for slot in range(3) for i in range(TILE // HDIM)],
+            [kv[slot, h, TILE + i * HDIM:TILE + (i + 1) * HDIM] for slot in slots for i in range(TILE // HDIM)],
             axis=1,
         )
-        alive = jnp.concatenate([live_rows[slot] for slot in range(3)], axis=1)
+        alive = jnp.concatenate([live_rows[slot] for slot in slots], axis=1)
         both = jnp.dot(jnp.concatenate([turned, alive], axis=0), expo, preferred_element_type=jnp.float32)
         return both[0:HDIM], top, both[HDIM:HDIM + 1]
 
@@ -138,14 +144,17 @@
         part_stat[which, h, 0:1] = top
         part_stat[which, h, 1:2] = total
 
-    def merged(which, h, ref):
+    def kept(which, h):
+        return part[which, h], part_stat[which, h, 0:1], part_stat[which, h, 1:2]
+
+    def merged(h, acc1, top1, total1, ref, there=True):
         stats = ref[h, HDIM:HDIM + STAT].astype(jnp.float32)
-        top2 = stats[0:1] + stats[1:2] + stats[2:3]
+        top2 = jnp.where(there, stats[0:1] + stats[1:2] + stats[2:3], top1)
         total2 = stats[3:4] + stats[4:5] + stats[5:6]
-        top1, total1 = part_stat[which, h, 0:1], part_stat[which, h, 1:2]
         top = jnp.maximum(top1, top2)
-        w1, w2 = jnp.exp2((top1 - top) * scale), jnp.exp2((top2 - top) * scale)
-        acc = part[which, h] * w1 + ref[h, 0:HDIM].astype(jnp.float32) * w2
+        w1 = jnp.exp2((top1 - top) * scale)
+        w2 = jnp.where(there, jnp.exp2((top2 - top) * scale), 0.0)
+        acc = acc1 * w1 + ref[h, 0:HDIM].astype(jnp.float32) * w2
         return acc, top, total1 * w1 + total2 * w2
 
     early, groups = min(AHEAD, group), heads // group
@@ -177,7 +186,14 @@
 
         @pl.when(jnp.logical_not(inner))
         def _():
-            remote(Q_X, g).start()
+            remote(Q_D, g).start()
+            remote(Q_B, g).start()
+
+    def relay_queries(g):
+        @pl.when(jnp.logical_not(inner))
+        def _():
+            remote(Q_B, g).wait_recv()
+            remote(Q_C, g).start()
 
     side_queries(0)
 
@@ -206,6 +222,28 @@
         def _():
             side_queries(g + 1)
 
+        @pl.when(t == 0)
+        def _():
+            relay_queries(0)
+
+        @pl.when(jnp.logical_and(t == g * group + group // 2, g + 1 < groups))
+        def _():
+            relay_queries(g + 1)
+
+        def opens(h):
+            return h == (h // group) * group
+
+        @pl.when(jnp.logical_and(inner, within(t - 1)))
+        def _():
+            h = t - 1
+
+            @pl.when(opens(h))
+            def _():
+                remote(Q_C, h // group).wait_recv()
+
+            packed_into(to_y, h, *attend(h, q_b[:, cut(h)], (0,)))
+            remote(O_Y, h).start()
+
         @pl.when(within(t - LAG))
         def _():
             h = t - LAG
@@ -216,16 +254,8 @@
                 kv[2, h, 0:TILE] = kv[0, h, 0:TILE]
                 kv[2, h, TILE:2 * TILE] = jnp.zeros((TILE, HDIM), jnp.bfloat16)
 
-            @pl.when(inner)
-            def _():
-                @pl.when(h == (h // group) * group)
-                def _():
-                    remote(Q_X, h // group).wait_recv()
-
-                packed_into(to_x, h, *attend(h, q_x[:, cut(h)]))
-                remote(O_X, h).start()
-
-            acc, top, total = attend(h, jnp.concatenate([q_own[:, cut(h)], q_p[:, cut(h)]], axis=0))
+            queries = jnp.concatenate([q_own[:, cut(h)], q_p[:, cut(h)]], axis=0)
+            acc, top, total = attend(h, queries, (0, 1, 2))
             keep(0, h, acc[:, 0:QROWS], top[:, 0:QROWS], total[:, 0:QROWS])
             for_p = acc[:, QROWS:], top[:, QROWS:], total[:, QROWS:]
 
@@ -238,18 +268,31 @@
             def _():
                 keep(1, h, *for_p)
 
+        @pl.when(jnp.logical_and(inner, within(t - 2)))
+        def _():
+            h = t - 2
+
+            @pl.when(opens(h))
+            def _():
+                remote(Q_D, h // group).wait_recv()
+
+            near = attend(h, q_a[:, cut(h)], (0, 1))
+            remote(O_Y, h).wait_recv()
+            packed_into(to_x, h, *merged(h, *near, from_y, third_there))
+            remote(O_X, h).start()
+
         @pl.when(jnp.logical_and(jnp.logical_not(inner), within(t - 2 * LAG)))
         def _():
             h = t - 2 * LAG
             remote(O_X, h).wait_recv()
-            packed_into(to_p, h, *merged(1, h, from_x))
+            packed_into(to_p, h, *merged(h, *kept(1, h), from_x))
             remote(O_P, h).start()
 
         @pl.when(t >= 3 * LAG)
         def _():
             h = t - 3 * LAG
             remote(O_P, h).wait_recv()
-            acc, top, total = merged(0, h, from_p)
+            acc, top, total = merged(h, *kept(0, h), from_p)
             done = jnp.transpose(acc / total)
             out[0, 0, :, cut(h)] = done.astype(out.dtype)
 
@@ -259,10 +302,13 @@
     @pl.when(inner)
     def _():
         remote(O_X).wait_send()
+        remote(O_Y).wait_send()
 
     @pl.when(jnp.logical_not(inner))
     def _():
-        remote(Q_X).wait_send()
+        remote(Q_D).wait_send()
+        remote(Q_B).wait_send()
+        remote(Q_C).wait_send()
 
 
 def shards(queries, keys, values, pad_counts):
@@ -278,19 +324,19 @@
         out_specs=pl.BlockSpec(memory_space=pltpu.VMEM),
         scratch_shapes=[
             pltpu.VMEM((3, heads, 2 * TILE, HDIM), bf16),
-            pltpu.VMEM((QROWS, width), bf16),
-            pltpu.VMEM((QROWS, width), bf16),
-            pltpu.VMEM((QROWS, width), bf16),
+        ]
+        + [pltpu.VMEM((QROWS, width), bf16)] * 5
+        + [
             pltpu.VMEM((2, heads, HDIM, QROWS), jnp.float32),
             pltpu.VMEM((2, heads, 8, QROWS), jnp.float32),
         ]
-        + [pltpu.VMEM((heads, HDIM + STAT, QROWS), bf16)] * 4
+        + [pltpu.VMEM((heads, HDIM + STAT, QROWS), bf16)] * 6
         + [pltpu.VMEM((TILE, width), bf16)] * 2
         + [
             pltpu.VMEM((3, STAT, TILE), bf16),
             pltpu.SemaphoreType.DMA((2, 3)),
-            pltpu.SemaphoreType.DMA((6,)),
-            pltpu.SemaphoreType.DMA((6, heads)),
+            pltpu.SemaphoreType.DMA((9,)),
+            pltpu.SemaphoreType.DMA((9, heads)),
         ],
         compiler_params=pltpu.CompilerParams(
             collective_id=0, has_side_effects=True, vmem_limit_bytes=60 * 1024 * 1024

time: 73.5 us -> 75.5 us (1.027)
  the two profiles are of different devices: /device:TPU:132 before, /device:TPU:158 now
where the time goes in v6:
time: 75.5 us; the launch traced here: 75.3 us
  Pallas kernels  73.5 us (97%)
  local copies, waits for them, and re-layouts  1.77 us (2%)
    pallas_call x1, Pallas kernels, shards(): pl.pallas_call(functools.partial(kernel, heads, rows // RT, frames, group...  73.5 us
    unnamed x1, local copies, waits for them, and re-layouts  1.77 us

profile of v6, /device:TPU:158, one launch (start us, length us, event | category | flops | bytes accessed | tf_op | source)
XLA Modules:
  0.0 75.3 jit_solution(14396994661183226336)
XLA Ops:
  0.0 73.5 %shard_map.46 = bf16[1,1,128,1536]{3,2,1,0:T(8,128)(2,1)} custom-call(bf16[1,1,128,1536]{3,2,1,0:T(8,128)(2,1)} %q_hbm.1, bf16[1,1,256,1536]{3,2,1,0:T(8,128)(2,1)} %k_hbm.1, bf16[1,1,256,1536]{3,2,1,0:T(8,128)(2,1)} %v_hbm.1, s32[16,32]{1,0:T(8,128)} %pads.1), custom_call_target="tpu_custom_call" | custom-call | tf_op jit(solution)/shard_map/pallas_call | solution.py:320
  73.5 1.8 %copy.6 = bf16[1,1,128,1536]{3,2,1,0:T(8,128)(2,1)} copy(bf16[1,1,128,1536]{3,2,1,0:T(8,128)(2,1)} %shard_map.46) | data formatting | bytes 786432

commit v7 on v5

--- a/solution.py
+++ b/solution.py
@@ -12,8 +12,8 @@
 QROWS = 128
 RT = 4
 LOG2E = 1.4426950408889634
-AHEAD = 3
-LAG = 3
+AHEAD = 4
+LAG = 2
 STAT = 16
 
 KV_X, KV_Y, Q_P, Q_X, O_P, O_X = range(6)
@@ -77,7 +77,7 @@
     def cut(h, count=1):
         return pl.ds(pl.multiple_of(h * HDIM, HDIM), count * HDIM)
 
-    def remote(kind, at=None):
+    def remote(kind, at=None, part_of=None):
         src, dst, device = {
             KV_X: (kv.at[0], kv.at[1], across),
             KV_Y: (kv.at[1], kv.at[2], onward),
@@ -88,10 +88,12 @@
         }[kind]
         if at is not None:
             index = (slice(None), cut(at * group, group)) if kind in (Q_P, Q_X) else (at,)
+            if part_of is not None:
+                index = (at, pl.ds(part_of * TILE, TILE))
             src, dst = src.at[index], dst.at[index]
         return pltpu.make_async_remote_copy(
             src_ref=src, dst_ref=dst, send_sem=send_sem.at[kind],
-            recv_sem=recv_sem.at[kind, 0 if at is None else at],
+            recv_sem=recv_sem.at[kind, 0 if at is None else heads if part_of == 1 else at],
             device_id=device, device_id_type=pl.DeviceIdType.MESH,
         )
 
@@ -102,6 +104,28 @@
     lane = lax.broadcasted_iota(jnp.int32, (STAT, TILE), 1)
     for slot, live in enumerate((live0, live1, live2)):
         live_rows[slot] = jnp.where(lane < live, 1.0, 0.0).astype(jnp.bfloat16)
+
+    def pairs(h, act):
+        last = h == heads - 1
+
+        @pl.when(jnp.logical_not(last))
+        def _():
+            act(None)
+
+        @pl.when(last)
+        def _():
+            act(0)
+            act(1)
+
+    def send_pairs(h):
+        pairs(h, lambda part_of: remote(KV_X, h, part_of).start())
+
+    def pass_pairs(h):
+        def act(part_of):
+            remote(KV_X, h, part_of).wait_recv()
+            remote(KV_Y, h, part_of).start()
+
+        pairs(h, act)
 
     def prepare(h):
         at = lax.broadcasted_iota(jnp.int32, (TILE, HDIM), 0)
@@ -158,7 +182,7 @@
     @pl.loop(0, early)
     def _(h):
         prepare(h)
-        remote(KV_X, h).start()
+        send_pairs(h)
 
     for copy in local_rest:
         copy.wait()
@@ -170,7 +194,7 @@
         prepare(h)
 
     for h in range(early, min(AHEAD, heads)):
-        remote(KV_X, h).start()
+        send_pairs(jnp.int32(h))
 
     def side_queries(g):
         remote(Q_P, g).wait_recv()
@@ -188,12 +212,11 @@
     def _(t):
         @pl.when(within(t))
         def _():
-            remote(KV_X, t).wait_recv()
-            remote(KV_Y, t).start()
+            pass_pairs(t)
 
         @pl.when(t + AHEAD < heads)
         def _():
-            remote(KV_X, t + AHEAD).start()
+            send_pairs(t + AHEAD)
 
         g = t // group
         fresh = t == g * group
@@ -209,12 +232,18 @@
         @pl.when(within(t - LAG))
         def _():
             h = t - LAG
-            remote(KV_Y, h).wait_recv()
+            pairs(h, lambda part_of: remote(KV_Y, h, part_of).wait_recv())
 
             @pl.when(jnp.logical_not(far_there))
             def _():
                 kv[2, h, 0:TILE] = kv[0, h, 0:TILE]
                 kv[2, h, TILE:2 * TILE] = jnp.zeros((TILE, HDIM), jnp.bfloat16)
+
+            def block(ref):
+                return ref[:, cut(h)]
+
+            def columns_of(i, results):
+                return [x[:, i * QROWS:(i + 1) * QROWS] for x in results]
 
             @pl.when(inner)
             def _():
@@ -222,21 +251,18 @@
                 def _():
                     remote(Q_X, h // group).wait_recv()
 
-                packed_into(to_x, h, *attend(h, q_x[:, cut(h)]))
+                results = attend(h, jnp.concatenate([block(q_own), block(q_p), block(q_x)], axis=0))
+                packed_into(to_x, h, *columns_of(2, results))
                 remote(O_X, h).start()
-
-            acc, top, total = attend(h, jnp.concatenate([q_own[:, cut(h)], q_p[:, cut(h)]], axis=0))
-            keep(0, h, acc[:, 0:QROWS], top[:, 0:QROWS], total[:, 0:QROWS])
-            for_p = acc[:, QROWS:], top[:, QROWS:], total[:, QROWS:]
-
-            @pl.when(inner)
-            def _():
-                packed_into(to_p, h, *for_p)
+                packed_into(to_p, h, *columns_of(1, results))
                 remote(O_P, h).start()
+                keep(0, h, *columns_of(0, results))
 
             @pl.when(jnp.logical_not(inner))
             def _():
-                keep(1, h, *for_p)
+                results = attend(h, jnp.concatenate([block(q_own), block(q_p)], axis=0))
+                keep(0, h, *columns_of(0, results))
+                keep(1, h, *columns_of(1, results))
 
         @pl.when(jnp.logical_and(jnp.logical_not(inner), within(t - 2 * LAG)))
         def _():
@@ -290,10 +316,10 @@
             pltpu.VMEM((3, STAT, TILE), bf16),
             pltpu.SemaphoreType.DMA((2, 3)),
             pltpu.SemaphoreType.DMA((6,)),
-            pltpu.SemaphoreType.DMA((6, heads)),
+            pltpu.SemaphoreType.DMA((6, heads + 1)),
         ],
         compiler_params=pltpu.CompilerParams(
-            collective_id=0, has_side_effects=True, vmem_limit_bytes=60 * 1024 * 1024
+            collective_id=0, has_side_effects=True, vmem_limit_bytes=53 * 1024 * 1024 + 400 * 1024
         ),
     )(queries, keys, values, pad_counts)
 

time: 73.5 us -> 72.2 us (0.982)
  the two profiles are of different devices: /device:TPU:132 before, /device:TPU:4 now
where the time goes in v7:
time: 72.2 us; the launch traced here: 72 us
  Pallas kernels  70.5 us (98%)
  local copies, waits for them, and re-layouts  1.44 us (2%)
    pallas_call x1, Pallas kernels, shards(): pl.pallas_call(functools.partial(kernel, heads, rows // RT, frames, group...  70.5 us
    unnamed x3, local copies, waits for them, and re-layouts  1.44 us

profile of v7, /device:TPU:4, one launch (start us, length us, event | category | flops | bytes accessed | tf_op | source)
XLA Modules:
  0.0 72.0 jit_solution(5205464986559938982)
XLA Ops:
  0.0 0.0 copy-start
  0.0 0.7 copy-done
  0.7 70.5 %shard_map.46 = bf16[1,1,128,1536]{3,2,1,0:T(8,128)(2,1)S(1)} custom-call(bf16[1,1,128,1536]{3,2,1,0:T(8,128)(2,1)} %q_hbm.1, bf16[1,1,256,1536]{3,2,1,0:T(8,128)(2,1)} %k_hbm.1, bf16[1,1,256,1536]{3,2,1,0:T(8,128)(2,1)} %v_hbm.1, s32[16,32]{1,0:T(8,128)S(1)} %copy-done), custom_call_target="tpu_custom_call" | custom-call | tf_op jit(solution)/shard_map/pallas_call | solution.py:300
  71.3 0.7 %copy.6 = bf16[1,1,128,1536]{3,2,1,0:T(8,128)(2,1)} copy(bf16[1,1,128,1536]{3,2,1,0:T(8,128)(2,1)S(1)} %shard_map.46) | data formatting | bytes 786432
Async XLA Ops:
  0.0 0.7 copy-start

commit v8 on v7

--- a/solution.py
+++ b/solution.py
@@ -93,7 +93,7 @@
             src, dst = src.at[index], dst.at[index]
         return pltpu.make_async_remote_copy(
             src_ref=src, dst_ref=dst, send_sem=send_sem.at[kind],
-            recv_sem=recv_sem.at[kind, 0 if at is None else heads if part_of == 1 else at],
+            recv_sem=recv_sem.at[kind, 0 if at is None else heads + at if part_of == 1 else at],
             device_id=device, device_id_type=pl.DeviceIdType.MESH,
         )
 
@@ -105,27 +105,14 @@
     for slot, live in enumerate((live0, live1, live2)):
         live_rows[slot] = jnp.where(lane < live, 1.0, 0.0).astype(jnp.bfloat16)
 
-    def pairs(h, act):
-        last = h == heads - 1
-
-        @pl.when(jnp.logical_not(last))
-        def _():
-            act(None)
-
-        @pl.when(last)
-        def _():
-            act(0)
-            act(1)
-
     def send_pairs(h):
-        pairs(h, lambda part_of: remote(KV_X, h, part_of).start())
+        for part_of in range(2):
+            remote(KV_X, h, part_of).start()
 
     def pass_pairs(h):
-        def act(part_of):
+        for part_of in range(2):
             remote(KV_X, h, part_of).wait_recv()
             remote(KV_Y, h, part_of).start()
-
-        pairs(h, act)
 
     def prepare(h):
         at = lax.broadcasted_iota(jnp.int32, (TILE, HDIM), 0)
@@ -194,7 +181,7 @@
         prepare(h)
 
     for h in range(early, min(AHEAD, heads)):
-        send_pairs(jnp.int32(h))
+        send_pairs(h)
 
     def side_queries(g):
         remote(Q_P, g).wait_recv()
@@ -232,7 +219,8 @@
         @pl.when(within(t - LAG))
         def _():
             h = t - LAG
-            pairs(h, lambda part_of: remote(KV_Y, h, part_of).wait_recv())
+            for part_of in range(2):
+                remote(KV_Y, h, part_of).wait_recv()
 
             @pl.when(jnp.logical_not(far_there))
             def _():
@@ -316,7 +304,7 @@
             pltpu.VMEM((3, STAT, TILE), bf16),
             pltpu.SemaphoreType.DMA((2, 3)),
             pltpu.SemaphoreType.DMA((6,)),
-            pltpu.SemaphoreType.DMA((6, heads + 1)),
+            pltpu.SemaphoreType.DMA((6, 2 * heads)),
         ],
         compiler_params=pltpu.CompilerParams(
             collective_id=0, has_side_effects=True, vmem_limit_bytes=53 * 1024 * 1024 + 400 * 1024

time: 72.2 us -> 72.7 us (level)
  no operation moved by 1% of the time
where the time goes in v8:
time: 72.7 us; the launch traced here: 72.6 us
  Pallas kernels  71.1 us (98%)
  local copies, waits for them, and re-layouts  1.44 us (2%)
    pallas_call x1, Pallas kernels, shards(): pl.pallas_call(functools.partial(kernel, heads, rows // RT, frames, group...  71.1 us

profile of v8, /device:TPU:4, one launch (start us, length us, event | category | flops | bytes accessed | tf_op | source)
XLA Modules:
  0.0 72.6 jit_solution(4299822796423901860)
XLA Ops:
  0.0 0.0 copy-start
  0.0 0.7 copy-done
  0.7 71.1 %shard_map.46 = bf16[1,1,128,1536]{3,2,1,0:T(8,128)(2,1)S(1)} custom-call(bf16[1,1,128,1536]{3,2,1,0:T(8,128)(2,1)} %q_hbm.1, bf16[1,1,256,1536]{3,2,1,0:T(8,128)(2,1)} %k_hbm.1, bf16[1,1,256,1536]{3,2,1,0:T(8,128)(2,1)} %v_hbm.1, s32[16,32]{1,0:T(8,128)S(1)} %copy-done), custom_call_target="tpu_custom_call" | custom-call | tf_op jit(solution)/shard_map/pallas_call | solution.py:288
  71.8 0.7 %copy.6 = bf16[1,1,128,1536]{3,2,1,0:T(8,128)(2,1)} copy(bf16[1,1,128,1536]{3,2,1,0:T(8,128)(2,1)S(1)} %shard_map.46) | data formatting | bytes 786432
Async XLA Ops:
  0.0 0.7 copy-start

commit v9 on v7

--- a/solution.py
+++ b/solution.py
@@ -12,7 +12,7 @@
 QROWS = 128
 RT = 4
 LOG2E = 1.4426950408889634
-AHEAD = 4
+AHEAD = (6, 2)
 LAG = 2
 STAT = 16
 
@@ -172,7 +172,8 @@
         acc = part[which, h] * w1 + ref[h, 0:HDIM].astype(jnp.float32) * w2
         return acc, top, total1 * w1 + total2 * w2
 
-    early, groups = min(AHEAD, group), heads // group
+    early, groups = min(max(AHEAD), group), heads // group
+    window = jnp.where(lax.rem(row, 2) == 0, AHEAD[0], AHEAD[1])
     pl.semaphore_wait(barrier, 5)
     local_first[0].wait()
     remote(Q_P, 0).start()
@@ -182,7 +183,10 @@
     @pl.loop(0, early)
     def _(h):
         prepare(h)
-        send_pairs(h)
+
+        @pl.when(h < window)
+        def _():
+            send_pairs(h)
 
     for copy in local_rest:
         copy.wait()
@@ -193,8 +197,11 @@
     def _(h):
         prepare(h)
 
-    for h in range(early, min(AHEAD, heads)):
-        send_pairs(jnp.int32(h))
+    @pl.loop(early, min(max(AHEAD), heads))
+    def _(h):
+        @pl.when(h < window)
+        def _():
+            send_pairs(h)
 
     def side_queries(g):
         remote(Q_P, g).wait_recv()
@@ -214,9 +221,9 @@
         def _():
             pass_pairs(t)
 
-        @pl.when(t + AHEAD < heads)
-        def _():
-            send_pairs(t + AHEAD)
+        @pl.when(t + window < heads)
+        def _():
+            send_pairs(t + window)
 
         g = t // group
         fresh = t == g * group

time: 72.2 us -> 76 us (1.053)
  Pallas kernels: 70.5 us -> 74.3 us
    pallas_call x1, Pallas kernels: 70.5 us -> 74.3 us  [shards(): pl.pallas_call(functools.partial(kernel, heads, rows // RT, frames, group...]
where the time goes in v9:
time: 76 us; the launch traced here: 75.8 us
  Pallas kernels  74.3 us (98%)
  local copies, waits for them, and re-layouts  1.44 us (2%)
    pallas_call x1, Pallas kernels, shards(): pl.pallas_call(functools.partial(kernel, heads, rows // RT, frames, group...  74.3 us

profile of v9, /device:TPU:4, one launch (start us, length us, event | category | flops | bytes accessed | tf_op | source)
XLA Modules:
  0.0 75.8 jit_solution(18105072439108767182)
XLA Ops:
  0.0 0.0 copy-start
  0.0 0.7 copy-done
  0.7 74.3 %shard_map.46 = bf16[1,1,128,1536]{3,2,1,0:T(8,128)(2,1)S(1)} custom-call(bf16[1,1,128,1536]{3,2,1,0:T(8,128)(2,1)} %q_hbm.1, bf16[1,1,256,1536]{3,2,1,0:T(8,128)(2,1)} %k_hbm.1, bf16[1,1,256,1536]{3,2,1,0:T(8,128)(2,1)} %v_hbm.1, s32[16,32]{1,0:T(8,128)S(1)} %copy-done), custom_call_target="tpu_custom_call" | custom-call | tf_op jit(solution)/shard_map/pallas_call | solution.py:307
  75.0 0.7 copy.6
Async XLA Ops:
  0.0 0.7 copy-start
